TPU v7x, 32 devices: a whole 2x2x4 slice. The times are simulated.
32 devices in a mesh: samp: 4 (over z), slab: 4 (over x, core), chan: 2 (over y).
Axes of the slice: x: 2, y: 2, z: 4, core: 2. Of those that a mesh axis runs over, the one named last changes fastest.
Arguments:
- volume: bfloat16 [4, 128, 8, 1024], P('samp', 'chan', 'slab'), may hold values from -6 to 6
- cotangent: bfloat16 [4, 128, 8, 1024], P('samp', 'chan', 'slab'), may hold values from -6 to 6
- filter_one: bfloat16 [128, 27, 128], P('chan'), may hold values from -0.109375 to 0.109375
- filter_two: bfloat16 [128, 27, 128], P('chan'), may hold values from -0.109375 to 0.109375
Outputs:
- block_out: bfloat16 [4, 128, 8, 1024], P('samp', 'chan', 'slab')
- grad_volume: bfloat16 [4, 128, 8, 1024], P('samp', 'chan', 'slab')
- grad_filter_one: float32 [128, 27, 128], P('chan')
- grad_filter_two: float32 [128, 27, 128], P('chan')
All inputs are finite; a program needn't handle non-finite values.
Results may differ from a plain program's by a relative error of at most 0.0033.
Values may be sent and summed in bfloat16 or wider, within the bound.
A program may use at most 64 MiB of HBM per device.

v0:
```python
import math

import jax
import jax.numpy as jnp
from jax import lax
from jax.sharding import PartitionSpec as P

SIDE = 32


plane_offsets = [(-1, -1), (-1, 0), (-1, 1), (0, -1), (0, 0), (0, 1), (1, -1), (1, 0), (1, 1)]


def extended(shard, sides, width):
    for axis, dim in sides:
        count, length = (lax.axis_size(axis), shard.shape[dim])
        up = [(i, (i + 1) % count) for i in range(count - 1)]
        down = [(j, i) for i, j in up]
        last = lax.slice_in_dim(shard, length - width, length, axis=dim)
        initial = lax.slice_in_dim(shard, 0, width, axis=dim)
        before = lax.ppermute(last, axis, up)
        after = lax.ppermute(initial, axis, down)
        shard = jnp.concatenate([before, shard, after], axis=dim)
    return shard


def plane_shift(values, row_off, col_off):
    length = values.shape[-1]
    widths = [(0, 0)] * (values.ndim - 1) + [(SIDE + 1, SIDE + 1)]
    padded = jnp.pad(values, widths)
    begin_at = SIDE + 1 + row_off * SIDE + col_off
    shifted_flat = padded[..., begin_at : begin_at + length]
    column = jnp.arange(length) % SIDE + col_off
    inside = (column >= 0) & (column < SIDE)
    return jnp.where(inside, shifted_flat, jnp.zeros_like(shifted_flat))


def convolve(padded, weight, inner):
    out_count, tap_count, in_count = weight.shape
    planes = padded.shape[1] - 2
    shifted = jnp.stack(
        [plane_shift(padded, row_off, col_off) for row_off, col_off in plane_offsets]
    )
    blocks = weight.reshape(out_count, 3, 9, in_count)
    summed = jnp.zeros((out_count, planes, inner), jnp.float32)
    for depth_off in range(3):
        summed = summed + jnp.einsum(
            "ojn,jndp->odp",
            blocks[:, depth_off],
            shifted[:, :, depth_off : depth_off + planes],
            preferred_element_type=jnp.float32,
        )
    return summed


def filter_grad(gradient, padded):
    out_count, planes, inner = gradient.shape
    shifted = jnp.stack(
        [plane_shift(gradient, -row_off, -col_off) for row_off, col_off in plane_offsets]
    )
    pieces = [
        jnp.einsum(
            "jodp,ndp->ojn",
            shifted,
            padded[:, depth_off : depth_off + planes],
            preferred_element_type=jnp.float32,
        )
        for depth_off in range(3)
    ]
    return jnp.stack(pieces, axis=1).reshape(out_count, 27, padded.shape[0])


def reverse_filter(weight):
    return jnp.transpose(weight[:, ::-1, :], (2, 1, 0))


def silu_slope(values):
    sigma = jax.nn.sigmoid(values)
    return sigma * (1.0 + values * (1.0 - sigma))


def depth_rim(values):
    return extended(values, (("slab", 1),), 1)


def per_device(volume, cotangent, filter_one, filter_two):
    source = volume[0]
    upstream = cotangent[0]
    cells = lax.axis_size("samp") * source.shape[1] * lax.axis_size("slab") * SIDE * SIDE
    norm_scale = 1.0 / math.sqrt(cells)
    inner = source.shape[2]
    source_pad = lax.all_gather(depth_rim(source), "chan", axis=0, tiled=True)
    pre_one = convolve(source_pad, filter_one, inner)
    hidden = (pre_one * jax.nn.sigmoid(pre_one)).astype(jnp.bfloat16)
    hidden_pad = lax.all_gather(depth_rim(hidden), "chan", axis=0, tiled=True)
    pre_two = convolve(hidden_pad, filter_two, inner)
    result = (source.astype(jnp.float32) + pre_two).astype(jnp.bfloat16)
    grad_two = filter_grad(upstream, hidden_pad)
    upstream_pad = depth_rim(upstream)
    filt_block = filter_two
    grad_hidden = lax.psum_scatter(
        convolve(upstream_pad, reverse_filter(filt_block), inner),
        "chan",
        scatter_dimension=0,
        tiled=True,
    )
    grad_pre = (grad_hidden * silu_slope(pre_one)).astype(jnp.bfloat16)
    grad_one = filter_grad(grad_pre, source_pad)
    pre_pad = depth_rim(grad_pre)
    filt_block = filter_one
    back = lax.psum_scatter(
        convolve(pre_pad, reverse_filter(filt_block), inner),
        "chan",
        scatter_dimension=0,
        tiled=True,
    )
    grad_input = (upstream.astype(jnp.float32) + back).astype(jnp.bfloat16)
    grad_one, grad_two = lax.psum((grad_one, grad_two), ("samp", "slab"))
    return (result[None], grad_input[None], grad_one * norm_scale, grad_two * norm_scale)


def solution(mesh):
    return jax.shard_map(
        per_device,
        mesh=mesh,
        in_specs=(
            P("samp", "chan", "slab", None),
            P("samp", "chan", "slab", None),
            P("chan", None, None),
            P("chan", None, None),
        ),
        out_specs=(
            P("samp", "chan", "slab", None),
            P("samp", "chan", "slab", None),
            P("chan", None, None),
            P("chan", None, None),
        ),
        check_vma=False,
    )
```

profile of v0, /device:TPU:0, one launch (start us, length us, event | category | flops | bytes accessed | tf_op | source)
XLA Modules:
  0.0 252.8 jit_solution(7685739371086647978)
XLA Ops:
  7.2 1.1 copy.83
  8.3 3.0 %collective-permute-start = (bf16[64,1,1024]{2,0,1:T(8,128)(2,1)S(1)}, bf16[64,1,1024]{2,0,1:T(8,128)(2,1)}, u32[]{:S(2)}, u32[]{:S(2)}) collective-permute-start(bf16[64,1,1024]{2,0,1:T(8,128)(2,1)S(1)} %get-tuple-element.20), channel_id=1, source_target_pairs={{0,2},{2,4},{4,6},{1,3},{3,5},{5,7},{8,10},{10,12},{12,14},{9,11},... | collective-permute-start | bytes 393224 | tf_op jit(solution)/shard_map/ppermute | solution.py:21
  11.3 1.3 collective-permute-start.1
  13.7 4.5 %collective-permute-start.4 = (bf16[64,1,1024]{2,0,1:T(8,128)(2,1)S(1)}, bf16[64,1,1024]{2,0,1:T(8,128)(2,1)S(1)}, u32[]{:S(2)}, u32[]{:S(2)}) collective-permute-start(bf16[64,1,1024]{2,0,1:T(8,128)(2,1)S(1)} %get-tuple-element.16), channel_id=1, source_target_pairs={{0,2},{2,4},{4,6},{1,3},{3,5},{5,7},{8,10},{10,12},{12,14},{9,11},... | collective-permute-start | bytes 393224 | tf_op jit(solution)/shard_map/ppermute | solution.py:21
  18.2 1.3 collective-permute-start.5
  23.0 1.8 select_dynamic-update-slice_fusion
  24.8 1.8 pad_maximum_fusion.2
  30.4 1.6 fusion.14
  32.3 19.6 %all-gather.3.cloned.1.call-done = bf16[128,4,1024]{2,0,1:T(8,128)(2,1)} async-done(((bf16[64,4,1024]{2,0,1:T(8,128)(2,1)}), bf16[128,4,1024]{2,0,1:T(8,128)(2,1)}) %all-gather.3.cloned.1.call-update) | async-done | bytes 1048592 | tf_op jit(solution)/shard_map/all_gather | solution.py:92
  51.9 1.8 bitcast_dynamic-update-slice_fusion.7
  53.7 1.8 bitcast_dynamic-update-slice_fusion.6
  62.1 12.3 %reduce-scatter.3.cloned.1.call-done = f32[64,2,1024]{2,0,1:T(8,128)} async-done(((f32[128,2,1024]{2,0,1:T(8,128)}), f32[64,2,1024]{2,0,1:T(8,128)}) %reduce-scatter.3.cloned.1.call-update) | async-done | bytes 524304 | tf_op jit(solution)/shard_map/reduce_scatter | solution.py:101
  74.5 1.3 multiply_convert_fusion
  76.1 1.7 collective-permute-start.2
  77.8 1.3 collective-permute-start.3
  83.3 4.3 %collective-permute-start.6 = (bf16[64,1,1024]{2,0,1:T(8,128)(2,1)S(1)}, bf16[64,1,1024]{2,0,1:T(8,128)(2,1)S(1)}, u32[]{:S(2)}, u32[]{:S(2)}) collective-permute-start(bf16[64,1,1024]{2,0,1:T(8,128)(2,1)S(1)} %get-tuple-element.14), channel_id=1, source_target_pairs={{0,2},{2,4},{4,6},{1,3},{3,5},{5,7},{8,10},{10,12},{12,14},{9,11},... | collective-permute-start | bytes 393224 | tf_op jit(solution)/shard_map/ppermute | solution.py:21
  87.6 1.3 collective-permute-start.7
  94.6 1.1 fusion.82
  95.7 1.1 fusion.80
  99.8 1.1 fusion.74
  101.9 1.1 fusion.70
  103.0 14.1 %all-gather.5.cloned.1.call-done = bf16[128,4,1024]{2,0,1:T(8,128)(2,1)} async-done(((bf16[64,4,1024]{2,0,1:T(8,128)(2,1)}), bf16[128,4,1024]{2,0,1:T(8,128)(2,1)}) %all-gather.5.cloned.1.call-update) | async-done | bytes 1048592 | tf_op jit(solution)/shard_map/all_gather | solution.py:95
  117.1 2.7 %convolution_bitcast_fusion.8 = f32[64,1,9,128]{3,0,2,1:T(8,128)S(1)} fusion(bf16[9,64,2,1024]{3,1,2,0:T(8,128)(2,1)} %get-tuple-element.22, bf16[128,4,1024]{2,0,1:T(8,128)(2,1)} %all-gather.5.cloned.1.call-done), kind=kOutput, calls=%fused_computation.43 | convolution fusion | flops 301989888 | bytes 3178496 | tf_op jit(solution)/shard_map/jodp,ndp->ojn/dot_general | solution.py:62
  119.8 2.6 %convolution_bitcast_fusion.7 = f32[64,1,9,128]{3,0,2,1:T(8,128)S(1)} fusion(bf16[9,64,2,1024]{3,1,2,0:T(8,128)(2,1)} %get-tuple-element.22, bf16[128,4,1024]{2,0,1:T(8,128)(2,1)} %all-gather.5.cloned.1.call-done), kind=kOutput, calls=%fused_computation.42 | convolution fusion | flops 301989888 | bytes 3178496 | tf_op jit(solution)/shard_map/jodp,ndp->ojn/dot_general | solution.py:62
  122.4 2.4 convolution_bitcast_fusion.6
  125.9 2.3 convolution_bitcast_fusion
  128.2 2.3 convolution_bitcast_fusion.1
  130.5 3.5 %fusion.17 = f32[128,2,1024]{2,0,1:T(8,128)} fusion(f32[2,1024,128]{1,2,0:T(8,128)S(1)} %convolution_bitcast_fusion, f32[2,1024,128]{1,2,0:T(8,128)S(1)} %convolution_bitcast_fusion.1, bf16[9,64,4,1024]{3,1,2,0:T(8,128)(2,1)} %fusion.70, bf16[128,3,9,64]{0,3,2,1:T(8,128)(2,1)S(1)} %bitcast.410), kind=kOutput, calls=%fused_computation.25 | convolution fusion | flops 302514176 | bytes 8011776 | tf_op jit(solution)/shard_map/ojn,jndp->odp/dot_general | solution.py:47
  142.9 79.8 %all-reduce.9.cloned.1.call-done = (f32[64,27,128]{2,0,1:T(8,128)}, f32[64,27,128]{2,0,1:T(8,128)}) async-done(((f32[64,27,128]{2,0,1:T(8,128)}, f32[64,27,128]{2,0,1:T(8,128)}), (f32[64,27,128]{2,0,1:T(8,128)}, f32[64,27,128]{2,0,1:T(8,128)})) %all-reduce.9.cloned.1.call-update) | async-done | bytes 1769488 | tf_op jit(solution)/shard_map/psum | solution.py:118
  222.7 2.9 %broadcast_multiply_fusion = (f32[64,27,128]{2,0,1:T(8,128)}, f32[64,27,128]{2,0,1:T(8,128)}) fusion(f32[64,27,128]{2,0,1:T(8,128)} %get-tuple-element.9, f32[64,27,128]{2,0,1:T(8,128)} %get-tuple-element.8), kind=kLoop, calls=%fused_computation.139 | loop fusion | flops 442368 | bytes 3538944 | tf_op jit(solution)/shard_map/mul | solution.py:119
  225.6 18.5 %reduce-scatter.5.cloned.1.call-done = f32[64,2,1024]{2,0,1:T(8,128)} async-done(((f32[128,2,1024]{2,0,1:T(8,128)}), f32[64,2,1024]{2,0,1:T(8,128)}) %reduce-scatter.5.cloned.1.call-update) | async-done | bytes 524304 | tf_op jit(solution)/shard_map/reduce_scatter | solution.py:111
  244.1 1.1 fusion.103
  (101 shorter events, 40.1 us)
Async XLA Ops:
  7.2 17.6 %copy-start.4 = (bf16[64,27,128]{2,0,1:T(8,128)(2,1)S(1)}, bf16[64,27,128]{2,0,1:T(8,128)(2,1)}, u32[]{:S(2)}) copy-start(bf16[64,27,128]{2,0,1:T(8,128)(2,1)} %param.7) | copy-start | bytes 1327108
  7.2 17.6 %copy-start.3 = (bf16[64,27,128]{2,0,1:T(8,128)(2,1)S(1)}, bf16[64,27,128]{2,0,1:T(8,128)(2,1)}, u32[]{:S(2)}) copy-start(bf16[64,27,128]{2,0,1:T(8,128)(2,1)} %param.6) | copy-start | bytes 1327108
  7.2 44.7 %all-gather.3.cloned.1.call-start = ((), (), s32[]{:S(2)}) async-start(), calls=%async_computation.2 | async-start | bytes 1572864 | tf_op jit(solution)/shard_map/all_gather | solution.py:92
  8.3 16.5 %collective-permute-start = (bf16[64,1,1024]{2,0,1:T(8,128)(2,1)S(1)}, bf16[64,1,1024]{2,0,1:T(8,128)(2,1)}, u32[]{:S(2)}, u32[]{:S(2)}) collective-permute-start(bf16[64,1,1024]{2,0,1:T(8,128)(2,1)S(1)} %get-tuple-element.20), channel_id=1, source_target_pairs={{0,2},{2,4},{4,6},{1,3},{3,5},{5,7},{8,10},{10,12},{12,14},{9,11},... | collective-permute-start | bytes 393224 | tf_op jit(solution)/shard_map/ppermute | solution.py:21
  11.3 13.5 %collective-permute-start.1 = (bf16[64,1,1024]{2,0,1:T(8,128)(2,1)S(1)}, bf16[64,1,1024]{2,0,1:T(8,128)(2,1)}, u32[]{:S(2)}, u32[]{:S(2)}) collective-permute-start(bf16[64,1,1024]{2,0,1:T(8,128)(2,1)S(1)} %get-tuple-element.21), channel_id=1, source_target_pairs={{2,0},{4,2},{6,4},{3,1},{5,3},{7,5},{10,8},{12,10},{14,12},{11,9},... | collective-permute-start | bytes 393224 | tf_op jit(solution)/shard_map/ppermute | solution.py:22
  13.7 13.1 %collective-permute-start.4 = (bf16[64,1,1024]{2,0,1:T(8,128)(2,1)S(1)}, bf16[64,1,1024]{2,0,1:T(8,128)(2,1)S(1)}, u32[]{:S(2)}, u32[]{:S(2)}) collective-permute-start(bf16[64,1,1024]{2,0,1:T(8,128)(2,1)S(1)} %get-tuple-element.16), channel_id=1, source_target_pairs={{0,2},{2,4},{4,6},{1,3},{3,5},{5,7},{8,10},{10,12},{12,14},{9,11},... | collective-permute-start | bytes 393224 | tf_op jit(solution)/shard_map/ppermute | solution.py:21
  18.2 8.6 %collective-permute-start.5 = (bf16[64,1,1024]{2,0,1:T(8,128)(2,1)S(1)}, bf16[64,1,1024]{2,0,1:T(8,128)(2,1)S(1)}, u32[]{:S(2)}, u32[]{:S(2)}) collective-permute-start(bf16[64,1,1024]{2,0,1:T(8,128)(2,1)S(1)} %get-tuple-element.17), channel_id=1, source_target_pairs={{2,0},{4,2},{6,4},{3,1},{5,3},{7,5},{10,8},{12,10},{14,12},{11,9},... | collective-permute-start | bytes 393224 | tf_op jit(solution)/shard_map/ppermute | solution.py:22
  26.7 47.8 %reduce-scatter.3.cloned.1.call-start = ((), (), s32[]{:S(2)}) async-start(), calls=%async_computation.4 | async-start | bytes 1572864 | tf_op jit(solution)/shard_map/reduce_scatter | solution.py:101
  32.1 85.0 %all-gather.5.cloned.1.call-start = ((), (), s32[]{:S(2)}) async-start(), calls=%async_computation.3 | async-start | bytes 1572864 | tf_op jit(solution)/shard_map/all_gather | solution.py:95
  51.9 3.6 %copy-start = (bf16[128,4,1024]{2,0,1:T(8,128)(2,1)S(1)}, bf16[128,4,1024]{2,0,1:T(8,128)(2,1)}, u32[]{:S(2)}) copy-start(bf16[128,4,1024]{2,0,1:T(8,128)(2,1)} %all-gather.3.cloned.1.call-done) | copy-start | bytes 3145732
  76.1 16.1 %collective-permute-start.2 = (bf16[64,1,1024]{2,0,1:T(8,128)(2,1)S(1)}, bf16[64,1,1024]{2,0,1:T(8,128)(2,1)S(1)}, u32[]{:S(2)}, u32[]{:S(2)}) collective-permute-start(bf16[64,1,1024]{2,0,1:T(8,128)(2,1)S(1)} %get-tuple-element.18), channel_id=1, source_target_pairs={{0,2},{2,4},{4,6},{1,3},{3,5},{5,7},{8,10},{10,12},{12,14},{9,11},... | collective-permute-start | bytes 393224 | tf_op jit(solution)/shard_map/ppermute | solution.py:21
  77.8 14.4 %collective-permute-start.3 = (bf16[64,1,1024]{2,0,1:T(8,128)(2,1)S(1)}, bf16[64,1,1024]{2,0,1:T(8,128)(2,1)S(1)}, u32[]{:S(2)}, u32[]{:S(2)}) collective-permute-start(bf16[64,1,1024]{2,0,1:T(8,128)(2,1)S(1)} %get-tuple-element.19), channel_id=1, source_target_pairs={{2,0},{4,2},{6,4},{3,1},{5,3},{7,5},{10,8},{12,10},{14,12},{11,9},... | collective-permute-start | bytes 393224 | tf_op jit(solution)/shard_map/ppermute | solution.py:22
  83.3 10.1 %collective-permute-start.6 = (bf16[64,1,1024]{2,0,1:T(8,128)(2,1)S(1)}, bf16[64,1,1024]{2,0,1:T(8,128)(2,1)S(1)}, u32[]{:S(2)}, u32[]{:S(2)}) collective-permute-start(bf16[64,1,1024]{2,0,1:T(8,128)(2,1)S(1)} %get-tuple-element.14), channel_id=1, source_target_pairs={{0,2},{2,4},{4,6},{1,3},{3,5},{5,7},{8,10},{10,12},{12,14},{9,11},... | collective-permute-start | bytes 393224 | tf_op jit(solution)/shard_map/ppermute | solution.py:21
  87.6 5.8 %collective-permute-start.7 = (bf16[64,1,1024]{2,0,1:T(8,128)(2,1)S(1)}, bf16[64,1,1024]{2,0,1:T(8,128)(2,1)S(1)}, u32[]{:S(2)}, u32[]{:S(2)}) collective-permute-start(bf16[64,1,1024]{2,0,1:T(8,128)(2,1)S(1)} %get-tuple-element.15), channel_id=1, source_target_pairs={{2,0},{4,2},{6,4},{3,1},{5,3},{7,5},{10,8},{12,10},{14,12},{11,9},... | collective-permute-start | bytes 393224 | tf_op jit(solution)/shard_map/ppermute | solution.py:22
  93.1 129.6 %all-reduce.9.cloned.1.call-start = ((), (), s32[]{:S(2)}) async-start(), calls=%async_computation.6 | async-start | bytes 3538944 | tf_op jit(solution)/shard_map/psum | solution.py:118
  117.1 5.3 %copy-start.1 = (bf16[128,4,1024]{2,0,1:T(8,128)(2,1)S(1)}, bf16[128,4,1024]{2,0,1:T(8,128)(2,1)}, u32[]{:S(2)}) copy-start(bf16[128,4,1024]{2,0,1:T(8,128)(2,1)} %all-gather.5.cloned.1.call-done) | copy-start | bytes 3145732
  125.9 118.3 %reduce-scatter.5.cloned.1.call-start = ((), (), s32[]{:S(2)}) async-start(), calls=%async_computation.5 | async-start | bytes 1572864 | tf_op jit(solution)/shard_map/reduce_scatter | solution.py:111
  139.0 2.0 copy-start.5
  140.9 103.2 %copy-start.2 = (bf16[1,64,2,1024]{3,2,1,0:T(2,128)(2,1)S(1)}, bf16[1,64,2,1024]{3,2,1,0:T(2,128)(2,1)}, u32[]{:S(2)}) copy-start(bf16[1,64,2,1024]{3,2,1,0:T(2,128)(2,1)} %param.5) | copy-start | bytes 786436
Sparse Core Ops, SparseCore 0:
  26.8 25.0 all-gather.2
  54.1 20.3 reduce-scatter.2
  93.2 23.7 all-gather.4
  126.0 96.6 all-reduce.8
  224.8 19.3 reduce-scatter.4
where the time goes:
time: 254 us; the launch traced here: 253 us
  waiting for transfers between devices  144 us (57%)
  other arithmetic  43.5 us (17%)
  matrix products  26.9 us (11%)
  starting transfers between devices  19.3 us (8%)
  between operations  14.4 us (6%)
  local copies, waits for them, and re-layouts  4.18 us (2%)
    psum x1, waiting for transfers between devices, per_device(): grad_one, grad_two = lax.psum((grad_one, grad_two), ('samp', 'slab'))  79.8 us
    unnamed x44, other arithmetic  29.4 us
    all_gather x1, waiting for transfers between devices, per_device(): source_pad = lax.all_gather(depth_rim(source), 'chan', axis=0, tiled=True)  19.6 us
    reduce_scatter x1, waiting for transfers between devices, per_device(): lax.psum_scatter(convolve(pre_pad, reverse_filter(filt_block), inner), 'c...  18.5 us
    dot_general x12, matrix products, convolve(): jnp.einsum('ojn,jndp->odp', blocks[:, depth_off], shifted[:, :, depth_off...  16.8 us
    all_gather x1, waiting for transfers between devices, per_device(): hidden_pad = lax.all_gather(depth_rim(hidden), 'chan', axis=0, tiled=True)  14.1 us
    ppermute x4, starting transfers between devices, extended(): before = lax.ppermute(last, axis, up)  13.6 us
    reduce_scatter x1, waiting for transfers between devices, per_device(): lax.psum_scatter(convolve(upstream_pad, reverse_filter(filt_block), inner...  12.3 us
  transfers between devices with their start and end apart: 13, of which 5 were waited for; matrix products, arithmetic and copies ran while one was open for 24% of the time, Pallas kernels for 0%

commit v1 on v0

v1 whole, which is shorter than its diff:
```python
import functools
import math

import jax
import jax.numpy as jnp
from jax import lax
from jax.experimental import pallas as pl
from jax.experimental.pallas import tpu as pltpu
from jax.sharding import PartitionSpec as P

SIDE = 32
CELLS = SIDE * SIDE
TILE = 512
MESH = pl.DeviceIdType.MESH
F32 = jnp.float32
BF16 = jnp.bfloat16

plane_offsets = [(-1, -1), (-1, 0), (-1, 1), (0, -1), (0, 0), (0, 1), (1, -1), (1, 0), (1, 1)]
SUM_TYPES = (F32, BF16)


def kernel(sizes, x_ref, ct_ref, w1_ref, w2_ref, w1t_ref, w2t_ref,
           out_ref, gv_ref, q1_ref, q2_ref,
           xpad, hpad, ctpad, gppad, wide, st_ct, st_gp, pre, gh, back,
           part_out, part_in, back_out, back_in,
           g1, g2, s1_1, r1_1, s2_1, r2_1, s1_2, r1_2, s2_2, r2_2,
           sx, rx, sxh, rxh, sct, rct, sgh, rgh, sh, rh, shh, rhh, sgp, rgp, sbk, rbk, sred, rred):
    nz, ns, nc, n, planes, shard, piece, norm_scale = sizes
    channels = n * nc
    zi, si, ci = lax.axis_index("samp"), lax.axis_index("slab"), lax.axis_index("chan")
    has_low, has_high = si > 0, si < ns - 1

    barrier = pltpu.get_barrier_semaphore()
    for k in range(1, nc):
        pl.semaphore_signal(barrier, inc=1, device_id={"chan": lax.rem(ci + k, nc)}, device_id_type=MESH)
    for k in range(1, ns):
        pl.semaphore_signal(barrier, inc=1, device_id={"slab": lax.rem(si + k, ns)}, device_id_type=MESH)
    for k in range(1, nz):
        pl.semaphore_signal(barrier, inc=1, device_id={"samp": lax.rem(zi + k, nz)}, device_id_type=MESH)
    pl.semaphore_wait(barrier, nc + ns + nz - 3)

    def rows_of(index):
        return pl.ds(pl.multiple_of(index * n, n), n)

    def send(src, dst, send_sem, recv_sem, axis, index):
        return pltpu.make_async_remote_copy(
            src_ref=src, dst_ref=dst, send_sem=send_sem, recv_sem=recv_sem,
            device_id={axis: index}, device_id_type=MESH)

    def halo_sends(padded, rows, ssem, rsem, slot):
        low = send(padded.at[1, rows], padded.at[planes + 1, rows], ssem.at[2 * slot], rsem.at[2 * slot], "slab", si - 1)
        high = send(padded.at[planes, rows], padded.at[0, rows], ssem.at[2 * slot + 1], rsem.at[2 * slot + 1], "slab", si + 1)
        return low, high

    def start_halo(*args):
        low, high = halo_sends(*args)
        pl.when(has_low)(low.start)
        pl.when(has_high)(high.start)

    def wait_halo(*args):
        low, high = halo_sends(*args)
        pl.when(has_high)(low.wait_recv)
        pl.when(has_low)(high.wait_recv)

    def finish_halo(*args):
        low, high = halo_sends(*args)
        pl.when(has_low)(low.wait_send)
        pl.when(has_high)(high.wait_send)

    own = rows_of(ci)
    everything = pl.ds(0, n)
    inside = pl.ds(1, planes)

    def gather_sends(padded, ssem, rsem):
        return [send(padded.at[inside, own], padded.at[inside, own], ssem.at[k - 1], rsem.at[k - 1],
                     "chan", lax.rem(ci + k, nc)) for k in range(1, nc)]

    def gather_arrivals(padded, ssem, rsem):
        out = []
        for k in range(1, nc):
            rows = rows_of(lax.rem(ci + nc - k, nc))
            out.append((k, rows, send(padded.at[inside, rows], padded.at[inside, rows], ssem.at[k - 1],
                                      rsem.at[k - 1], "chan", lax.rem(ci + k, nc))))
        return out

    def zero_edges(padded):
        @pl.when(jnp.logical_not(has_low))
        def _():
            padded[0] = jnp.zeros(padded.shape[1:], BF16)

        @pl.when(jnp.logical_not(has_high))
        def _():
            padded[planes + 1] = jnp.zeros(padded.shape[1:], BF16)

    cell = lax.broadcasted_iota(jnp.int32, (1, CELLS), 1)
    row, column = cell // SIDE, cell % SIDE
    masks = []
    for b, c in plane_offsets:
        ok = (row + b >= 0) & (row + b < SIDE) & (column + c >= 0) & (column + c < SIDE)
        masks.append(jnp.where(ok, 1.0, 0.0).astype(F32))

    def build(stack, padded, plane):
        count = padded.shape[1]

        def body(step, _):
            start = pl.multiple_of(step * 16, 16)
            values = padded[plane, pl.ds(start, 16), :]
            wide_values = values.astype(F32)
            for j, (b, c) in enumerate(plane_offsets):
                shift = (-(SIDE * b + c)) % CELLS
                if shift == 0:
                    moved = values
                else:
                    moved = (pltpu.roll(wide_values, shift, 1) * masks[j]).astype(BF16)
                stack[plane, pl.ds(pl.multiple_of(j * count + step * 16, 16), 16), :] = moved
            return 0

        lax.fori_loop(0, count // 16, body, 0)

    def convolve(weight, stack, emit):
        tiles = CELLS // TILE

        def body(step, _):
            d = step // tiles
            cols = pl.ds(pl.multiple_of((step % tiles) * TILE, TILE), TILE)
            total = None
            for a in range(3):
                term = jnp.dot(weight(a), stack[d + a, :, cols], preferred_element_type=F32)
                total = term if total is None else total + term
            emit(d, cols, total)
            return 0

        lax.fori_loop(0, planes * tiles, body, 0)

    def filter_grad(total_ref, stack, padded):
        count = stack.shape[1]
        for a in range(3):
            total = None
            for d in range(planes):
                term = lax.dot_general(stack[d + 1], padded[d + a], (((1,), (1,)), ((), ())),
                                       preferred_element_type=F32)
                total = term if total is None else total + term
            total_ref[pl.ds(a * count, count), :] = total
        rest = ns * shard - 3 * count
        if rest:
            total_ref[pl.ds(3 * count, rest), :] = jnp.zeros((rest, channels), F32)

    xpad[inside, own, :] = x_ref[...]
    for copy in gather_sends(xpad, sx, rx):
        copy.start()
    start_halo(xpad, own, sxh, rxh, 0)
    ctpad[inside] = ct_ref[...]
    start_halo(ctpad, everything, sct, rct, 0)

    zero_edges(ctpad)
    zero_edges(xpad)
    for plane in range(1, planes + 1):
        build(st_ct, ctpad, plane)
    wait_halo(ctpad, everything, sct, rct, 0)
    build(st_ct, ctpad, 0)
    build(st_ct, ctpad, planes + 1)

    def reverse_parts(weight_t, stack, mine, outgoing, incoming, ssem, rsem):
        for k in range(1, nc):
            target = lax.rem(ci + k, nc)

            def emit(d, cols, total, k=k):
                outgoing[k - 1, d, :, cols] = total.astype(outgoing.dtype)

            convolve(lambda a: weight_t[a, rows_of(target), :], stack, emit)
            send(outgoing.at[k - 1], incoming.at[k - 1], ssem.at[k - 1], rsem.at[k - 1], "chan", target).start()

        def keep(d, cols, total):
            mine[d, :, cols] = total

        convolve(lambda a: weight_t[a, own, :], stack, keep)

    def part_copies(outgoing, incoming, ssem, rsem):
        return [send(outgoing.at[k - 1], incoming.at[k - 1], ssem.at[k - 1], rsem.at[k - 1],
                     "chan", lax.rem(ci + k, nc)) for k in range(1, nc)]

    reverse_parts(w2t_ref, st_ct, gh, part_out, part_in, sgh, rgh)

    for k, rows, copy in gather_arrivals(xpad, sx, rx):
        copy.wait_recv()
        start_halo(xpad, rows, sxh, rxh, k)
    for plane in range(1, planes + 1):
        build(wide, xpad, plane)
    for k in range(nc):
        wait_halo(xpad, rows_of(lax.rem(ci + nc - k, nc)), sxh, rxh, k)
    build(wide, xpad, 0)
    build(wide, xpad, planes + 1)

    def hidden_out(d, cols, total):
        pre[d, :, cols] = total
        hpad[d + 1, own, cols] = (total * jax.nn.sigmoid(total)).astype(BF16)

    convolve(lambda a: w1_ref[a], wide, hidden_out)
    for copy in gather_sends(hpad, sh, rh):
        copy.start()
    start_halo(hpad, own, shh, rhh, 0)
    zero_edges(hpad)
    zero_edges(gppad)

    for copy in part_copies(part_out, part_in, sgh, rgh):
        copy.wait_recv()

    def slope(step, _):
        d = step // (n // 16)
        rows = pl.ds(pl.multiple_of((step % (n // 16)) * 16, 16), 16)
        total = gh[d, rows, :]
        for k in range(nc - 1):
            total = total + part_in[k, d, rows, :].astype(F32)
        values = pre[d, rows, :]
        sigma = jax.nn.sigmoid(values)
        gppad[d + 1, rows, :] = (total * (sigma * (1.0 + values * (1.0 - sigma)))).astype(BF16)
        return 0

    lax.fori_loop(0, planes * (n // 16), slope, 0)
    start_halo(gppad, everything, sgp, rgp, 0)
    for plane in range(1, planes + 1):
        build(st_gp, gppad, plane)
    filter_grad(g1, st_gp, xpad)

    def shard_rows(index):
        return pl.ds(pl.multiple_of(index * shard, 16), shard)

    def piece_rows(slab_index, samp_index):
        return pl.ds(pl.multiple_of(slab_index * shard + samp_index * piece, 16), piece)

    class Reduction:
        def __init__(self, which, total, out1, in1, out2, in2, result):
            self.total, self.out1, self.in1, self.out2, self.in2, self.result = total, out1, in1, out2, in2, result
            base = which * 2 * (ns + nz)
            self.base1, self.base2 = base, base + ns
            self.base3, self.base4 = base + ns + nz, base + ns + 2 * nz

        def slab_copies(self):
            return [send(self.out1.at[k - 1], self.in1.at[k - 1], sred.at[self.base1 + k], rred.at[self.base1 + k],
                         "slab", lax.rem(si + k, ns)) for k in range(1, ns)]

        def samp_copies(self):
            return [send(self.out2.at[k - 1], self.in2.at[k - 1], sred.at[self.base2 + k], rred.at[self.base2 + k],
                         "samp", lax.rem(zi + k, nz)) for k in range(1, nz)]

        def samp_gather(self, back_by):
            out = []
            for k in range(1, nz):
                rows = piece_rows(si, lax.rem(zi + nz - k, nz) if back_by else zi)
                out.append(send(self.result.at[rows], self.result.at[rows], sred.at[self.base3 + k],
                                rred.at[self.base3 + k], "samp", lax.rem(zi + k, nz)))
            return out

        def slab_gather(self, back_by):
            out = []
            for k in range(1, ns):
                rows = shard_rows(lax.rem(si + ns - k, ns) if back_by else si)
                out.append(send(self.result.at[rows], self.result.at[rows], sred.at[self.base4 + k],
                                rred.at[self.base4 + k], "slab", lax.rem(si + k, ns)))
            return out

        def one(self):
            copies = self.slab_copies()
            for k in range(1, ns):
                rows = shard_rows(lax.rem(si + k, ns))
                self.out1[k - 1] = self.total[rows, :].astype(self.out1.dtype)
                copies[k - 1].start()

        def two(self):
            for copy in self.slab_copies():
                copy.wait_recv()
            rows = shard_rows(si)
            summed = self.total[rows, :]
            for k in range(ns - 1):
                summed = summed + self.in1[k].astype(F32)
            self.total[rows, :] = summed
            copies = self.samp_copies()
            for k in range(1, nz):
                self.out2[k - 1] = self.total[piece_rows(si, lax.rem(zi + k, nz)), :].astype(self.out2.dtype)
                copies[k - 1].start()

        def three(self):
            for copy in self.samp_copies():
                copy.wait_recv()
            rows = piece_rows(si, zi)
            summed = self.total[rows, :]
            for k in range(nz - 1):
                summed = summed + self.in2[k].astype(F32)
            self.result[rows, :] = (summed * norm_scale).astype(BF16)
            for copy in self.samp_gather(False):
                copy.start()

        def four(self):
            for copy in self.samp_gather(True):
                copy.wait_recv()
            for copy in self.slab_gather(False):
                copy.start()

        def five(self):
            for copy in self.slab_gather(True):
                copy.wait_recv()

        def finish(self):
            for copy in self.slab_copies() + self.samp_copies() + self.samp_gather(False) + self.slab_gather(False):
                copy.wait_send()

    first = Reduction(0, g1, s1_1, r1_1, s2_1, r2_1, q1_ref)
    second = Reduction(1, g2, s1_2, r1_2, s2_2, r2_2, q2_ref)
    first.one()

    wait_halo(gppad, everything, sgp, rgp, 0)
    build(st_gp, gppad, 0)
    build(st_gp, gppad, planes + 1)
    reverse_parts(w1t_ref, st_gp, back, back_out, back_in, sbk, rbk)

    for k, rows, copy in gather_arrivals(hpad, sh, rh):
        copy.wait_recv()
        start_halo(hpad, rows, shh, rhh, k)
    first.two()
    for plane in range(1, planes + 1):
        build(wide, hpad, plane)
    for k in range(nc):
        wait_halo(hpad, rows_of(lax.rem(ci + nc - k, nc)), shh, rhh, k)
    filter_grad(g2, st_ct, hpad)
    second.one()
    first.three()
    build(wide, hpad, 0)
    build(wide, hpad, planes + 1)

    def block(d, cols, total):
        out_ref[d, :, cols] = (x_ref[d, :, cols].astype(F32) + total).astype(BF16)

    convolve(lambda a: w2_ref[a], wide, block)
    second.two()
    first.four()

    for copy in part_copies(back_out, back_in, sbk, rbk):
        copy.wait_recv()

    def volume_grad(step, _):
        d = step // (n // 16)
        rows = pl.ds(pl.multiple_of((step % (n // 16)) * 16, 16), 16)
        total = back[d, rows, :]
        for k in range(nc - 1):
            total = total + back_in[k, d, rows, :].astype(F32)
        gv_ref[d, rows, :] = (ct_ref[d, rows, :].astype(F32) + total).astype(BF16)
        return 0

    lax.fori_loop(0, planes * (n // 16), volume_grad, 0)
    second.three()
    second.four()
    first.five()
    second.five()

    for copy in gather_sends(xpad, sx, rx) + gather_sends(hpad, sh, rh):
        copy.wait_send()
    for copy in part_copies(part_out, part_in, sgh, rgh) + part_copies(back_out, back_in, sbk, rbk):
        copy.wait_send()
    for k in range(nc):
        rows = rows_of(lax.rem(ci + nc - k, nc))
        finish_halo(xpad, rows, sxh, rxh, k)
        finish_halo(hpad, rows, shh, rhh, k)
    finish_halo(ctpad, everything, sct, rct, 0)
    finish_halo(gppad, everything, sgp, rgp, 0)
    first.finish()
    second.finish()


def per_device(volume, cotangent, filter_one, filter_two):
    n, planes, cells = volume.shape[1:]
    nz, ns, nc = (lax.axis_size(axis) for axis in ("samp", "slab", "chan"))
    channels = n * nc
    norm_scale = 1.0 / math.sqrt(nz * planes * ns * cells)
    unit = 16 * ns * nz
    rows = -(-27 * n // unit) * unit
    shard, piece = rows // ns, rows // ns // nz

    def forward(weight):
        return jnp.transpose(weight.reshape(n, 3, 9 * channels), (1, 0, 2))

    def backward(weight):
        flipped = weight[:, ::-1, :].reshape(n, 3, 9, channels)
        return jnp.transpose(flipped, (1, 3, 2, 0)).reshape(3, channels, 9 * n)

    x = jnp.transpose(volume[0], (1, 0, 2))
    ct = jnp.transpose(cotangent[0], (1, 0, 2))
    vmem = pl.BlockSpec(memory_space=pltpu.VMEM)
    padded = planes + 2
    dma = pltpu.SemaphoreType.DMA

    def reduction_buffers(dtype):
        return [pltpu.VMEM((ns - 1, shard, channels), dtype)] * 2 + [pltpu.VMEM((nz - 1, piece, channels), dtype)] * 2

    scratch = [
        pltpu.VMEM((padded, channels, cells), BF16),
        pltpu.VMEM((padded, channels, cells), BF16),
        pltpu.VMEM((padded, n, cells), BF16),
        pltpu.VMEM((padded, n, cells), BF16),
        pltpu.VMEM((padded, 9 * channels, cells), BF16),
        pltpu.VMEM((padded, 9 * n, cells), BF16),
        pltpu.VMEM((padded, 9 * n, cells), BF16),
        pltpu.VMEM((planes, n, cells), F32),
        pltpu.VMEM((planes, n, cells), F32),
        pltpu.VMEM((planes, n, cells), F32),
    ] + [pltpu.VMEM((nc - 1, planes, n, cells), BF16)] * 4 + [
        pltpu.VMEM((rows, channels), F32),
        pltpu.VMEM((rows, channels), F32),
    ] + reduction_buffers(SUM_TYPES[0]) + reduction_buffers(SUM_TYPES[1]) + [
        dma((nc,)), dma((nc,)), dma((2 * nc,)), dma((2 * nc,)),
        dma((2,)), dma((2,)), dma((nc,)), dma((nc,)),
        dma((nc,)), dma((nc,)), dma((2 * nc,)), dma((2 * nc,)),
        dma((2,)), dma((2,)), dma((nc,)), dma((nc,)),
        dma((4 * (ns + nz),)), dma((4 * (ns + nz),)),
    ]
    sizes = (nz, ns, nc, n, planes, shard, piece, norm_scale)
    block, grad_volume, one, two = pl.pallas_call(
        functools.partial(kernel, sizes),
        out_shape=(
            jax.ShapeDtypeStruct((planes, n, cells), BF16),
            jax.ShapeDtypeStruct((planes, n, cells), BF16),
            jax.ShapeDtypeStruct((rows, channels), BF16),
            jax.ShapeDtypeStruct((rows, channels), BF16),
        ),
        in_specs=[vmem] * 6,
        out_specs=(vmem,) * 4,
        scratch_shapes=scratch,
        compiler_params=pltpu.CompilerParams(
            collective_id=0, has_side_effects=True, vmem_limit_bytes=56 * 1024 * 1024),
        cost_estimate=pl.CostEstimate(
            flops=6 * 2 * planes * cells * n * 27 * channels, bytes_accessed=8 << 20, transcendentals=planes * n * cells),
        name="residual_pair",
    )(x, ct, forward(filter_one), forward(filter_two), backward(filter_one), backward(filter_two))

    def filter_out(values):
        values = values[: 27 * n].reshape(3, 9, n, channels)[:, ::-1]
        return jnp.transpose(values, (2, 0, 1, 3)).reshape(n, 27, channels).astype(F32)

    return (
        jnp.transpose(block, (1, 0, 2))[None],
        jnp.transpose(grad_volume, (1, 0, 2))[None],
        filter_out(one),
        filter_out(two),
    )


def solution(mesh):
    return jax.shard_map(
        per_device,
        mesh=mesh,
        in_specs=(
            P("samp", "chan", "slab", None),
            P("samp", "chan", "slab", None),
            P("chan", None, None),
            P("chan", None, None),
        ),
        out_specs=(
            P("samp", "chan", "slab", None),
            P("samp", "chan", "slab", None),
            P("chan", None, None),
            P("chan", None, None),
        ),
        check_vma=False,
    )
```

time: 254 us -> 77.7 us (0.31)
  waiting for transfers between devices: 144 us -> 0 us
  Pallas kernels: 0 us -> 64.9 us
  other arithmetic: 43.5 us -> 2.02 us
  matrix products: 26.9 us -> 0 us
  starting transfers between devices: 19.3 us -> 0 us
  between operations: 14.4 us -> 0.73 us
  local copies, waits for them, and re-layouts: 4.18 us -> 9.21 us
    psum x1 -> x0, waiting for transfers between devices: 79.8 us -> none  [per_device(): grad_one, grad_two = lax.psum((grad_one, grad_two), ('samp', 'slab'))]
    pallas_call x0 -> x1, Pallas kernels: none -> 64.9 us  [per_device(): pl.pallas_call(functools.partial(kernel, sizes), out_shape=(jax.ShapeDtyp...]
    all_gather x2 -> x0, waiting for transfers between devices: 33.7 us -> none  [the longest x1 19.6 us: per_device(): source_pad = lax.all_gather(depth_rim(source), 'chan', axis=0, tiled=True)]
    reduce_scatter x2 -> x0, waiting for transfers between devices: 30.8 us -> none  [the longest x1 18.5 us: per_device(): lax.psum_scatter(convolve(pre_pad, reverse_filter(filt_block), inner), 'c...]
    unnamed x44 -> x0, other arithmetic: 29.4 us -> none
    dot_general x18 -> x0, matrix products: 26.9 us -> none  [the longest x12 16.8 us: convolve(): jnp.einsum('ojn,jndp->odp', blocks[:, depth_off], shifted[:, :, depth_off...]
    ppermute x8 -> x0, starting transfers between devices: 18.7 us -> none  [the longest x4 13.6 us: extended(): before = lax.ppermute(last, axis, up)]
    another operation x8 -> x0, other arithmetic: 5.49 us -> none  [the longest x4 2.46 us: convolve(): jnp.stack([plane_shift(padded, row_off, col_off) for row_off, col_off in...]
  transfers between devices with their start and end apart: 13 -> 0, of which waited for: 5 -> 0; matrix products, arithmetic and copies ran while one was open for 24% -> 0% of each run, Pallas kernels for 0% -> 0%
where the time goes in v1:
time: 77.7 us; the launch traced here: 76.9 us
  Pallas kernels  64.9 us (84%)
  local copies, waits for them, and re-layouts  9.21 us (12%)
  other arithmetic  2.02 us (3%)
    pallas_call x1, Pallas kernels, per_device(): pl.pallas_call(functools.partial(kernel, sizes), out_shape=(jax.ShapeDtyp...  64.9 us
    unnamed x18, local copies, waits for them, and re-layouts  3.66 us
    convert_element_type x2, other arithmetic, filter_out(): jnp.transpose(values, (2, 0, 1, 3)).reshape(n, 27, channels).astype(F32)  2.02 us
    reshape x2, local copies, waits for them, and re-layouts, backward(): return jnp.transpose(flipped, (1, 3, 2, 0)).reshape(3, channels, 9 * n)  1.99 us

profile of v1, /device:TPU:0, one launch (start us, length us, event | category | flops | bytes accessed | tf_op | source)
XLA Modules:
  0.0 76.9 jit_solution(13875131662022126712)
XLA Ops:
  0.6 1.0 %rev.12 = bf16[64,27,128]{2,0,1:T(8,128)(2,1)S(1)} reverse(bf16[64,27,128]{2,0,1:T(8,128)(2,1)} %param.6), dimensions={1} | reverse | bytes 884736 | tf_op jit(solution)/shard_map/rev | solution.py:382
  1.7 0.0 copy-start.1
  1.7 1.0 %copy.20.w1t_ref = bf16[3,128,576]{2,1,0:T(8,128)(2,1)} copy(bf16[3,128,576]{1,2,0:T(8,128)(2,1)S(1)} %bitcast.36) | data formatting | bytes 884736 | tf_op jit(solution)/shard_map/reshape | solution.py:383
  2.7 0.0 copy-done.1
  2.7 0.0 copy-start
  2.7 1.0 %copy.21.w2t_ref = bf16[3,128,576]{2,1,0:T(8,128)(2,1)} copy(bf16[3,128,576]{1,2,0:T(8,128)(2,1)S(1)} %bitcast.37) | data formatting | bytes 884736 | tf_op jit(solution)/shard_map/reshape | solution.py:383
  3.7 0.0 copy-done
  3.7 0.3 copy.16
  4.0 0.2 reshape.38
  4.3 0.3 copy.18
  4.6 0.2 reshape.39
  4.8 0.0 copy-start.5
  4.8 0.0 copy-start.6
  4.8 1.1 %copy_bitcast_fusion = (bf16[3,64,1152]{2,1,0:T(8,128)(2,1)}, bf16[3,64,1152]{2,1,0:T(8,128)(2,1)}) fusion(bf16[64,3,1152]{2,1,0:T(4,128)(2,1)S(1)} %reshape.39, bf16[64,3,1152]{2,1,0:T(4,128)(2,1)S(1)} %reshape.38), kind=kLoop, calls=%fused_computation | loop fusion | bytes 1769472 | tf_op jit(solution)/shard_map/transpose | solution.py:379
  5.9 0.0 copy-done.5
  5.9 0.0 copy-done.6
  5.9 0.9 %copy_bitcast_fusion.2 = (bf16[2,64,1024]{2,1,0:T(8,128)(2,1)}, bf16[2,64,1024]{2,1,0:T(8,128)(2,1)}) fusion(bf16[1,64,2,1024]{3,2,1,0:T(2,128)(2,1)S(1)} %copy-done.5, bf16[1,64,2,1024]{3,2,1,0:T(2,128)(2,1)S(1)} %copy-done.6), kind=kLoop, calls=%fused_computation.4 | loop fusion | bytes 1048576 | tf_op jit(solution)/shard_map/transpose | solution.py:386
  6.8 64.9 %residual_pair.1 = (bf16[2,64,1024]{2,1,0:T(8,128)(2,1)}, bf16[2,64,1024]{2,1,0:T(8,128)(2,1)}, bf16[1792,128]{1,0:T(8,128)(2,1)}, bf16[1792,128]{1,0:T(8,128)(2,1)}) custom-call(bf16[2,64,1024]{2,1,0:T(8,128)(2,1)} %get-tuple-element.23.x_ref, bf16[2,64,1024]{2,1,0:T(8,128)(2,1)} %get-tuple-element.22.ct_ref, ...), custom_call_target="tpu_custom_call" | custom-call | flops 5435817984 | bytes 8388608 | tf_op jit(solution)/shard_map/residual_pair/pallas_call | solution.py:416
  71.7 0.0 copy-start.4
  71.7 0.0 copy-start.3
  71.7 2.0 %copy.22 = bf16[1,64,2,1024]{3,2,1,0:T(2,128)(2,1)} copy(bf16[1,64,2,1024]{3,1,2,0:T(8,128)(2,1)} %bitcast.43) | data formatting | bytes 524288
  73.7 0.0 copy-done.4
  73.7 1.0 %copy.23 = bf16[1,64,2,1024]{3,2,1,0:T(2,128)(2,1)} copy(bf16[1,64,2,1024]{3,1,2,0:T(8,128)(2,1)S(1)} %bitcast.42) | data formatting | bytes 524288
  74.7 0.0 copy-done.3
  74.7 0.0 copy-start.2
  74.8 1.0 %reverse_convert_fusion.1 = f32[3,9,64,128]{3,2,1,0:T(8,128)} fusion(bf16[3,9,64,128]{3,2,1,0:T(8,128)(2,1)S(1)} %bitcast.38), kind=kLoop, calls=%fused_computation.3 | loop fusion | flops 221184 | bytes 1327104 | tf_op jit(solution)/shard_map/convert_element_type | solution.py:436
  75.8 0.0 copy-done.2
  75.8 1.0 %reverse_convert_fusion = f32[3,9,64,128]{3,2,1,0:T(8,128)} fusion(bf16[3,9,64,128]{3,2,1,0:T(8,128)(2,1)S(1)} %bitcast.39), kind=kLoop, calls=%fused_computation.2 | loop fusion | flops 221184 | bytes 1327104 | tf_op jit(solution)/shard_map/convert_element_type | solution.py:436
  (3 shorter events, 0.1 us)
Async XLA Ops:
  1.7 1.0 %copy-start.1 = (bf16[64,27,128]{2,0,1:T(8,128)(2,1)S(1)}, bf16[64,27,128]{2,0,1:T(8,128)(2,1)}, u32[]{:S(2)}) copy-start(bf16[64,27,128]{2,0,1:T(8,128)(2,1)} %param.7) | copy-start | bytes 1327108
  2.7 1.0 %copy-start = (bf16[64,27,128]{2,0,1:T(8,128)(2,1)S(1)}, bf16[64,27,128]{2,0,1:T(8,128)(2,1)}, u32[]{:S(2)}) copy-start(bf16[64,27,128]{2,0,1:T(8,128)(2,1)} %param.6) | copy-start | bytes 1327108
  4.8 1.1 %copy-start.5 = (bf16[1,64,2,1024]{3,2,1,0:T(2,128)(2,1)S(1)}, bf16[1,64,2,1024]{3,2,1,0:T(2,128)(2,1)}, u32[]{:S(2)}) copy-start(bf16[1,64,2,1024]{3,2,1,0:T(2,128)(2,1)} %param.5) | copy-start | bytes 786436
  4.8 1.1 %copy-start.6 = (bf16[1,64,2,1024]{3,2,1,0:T(2,128)(2,1)S(1)}, bf16[1,64,2,1024]{3,2,1,0:T(2,128)(2,1)}, u32[]{:S(2)}) copy-start(bf16[1,64,2,1024]{3,2,1,0:T(2,128)(2,1)} %param.4) | copy-start | bytes 786436
  71.7 2.0 %copy-start.4 = (bf16[2,64,1024]{2,1,0:T(8,128)(2,1)S(1)}, bf16[2,64,1024]{2,1,0:T(8,128)(2,1)}, u32[]{:S(2)}) copy-start(bf16[2,64,1024]{2,1,0:T(8,128)(2,1)} %get-tuple-element.9) | copy-start | bytes 786436
  71.7 3.0 %copy-start.3 = (bf16[1792,128]{1,0:T(8,128)(2,1)S(1)}, bf16[1792,128]{1,0:T(8,128)(2,1)}, u32[]{:S(2)}) copy-start(bf16[1792,128]{1,0:T(8,128)(2,1)} %get-tuple-element.10) | copy-start | bytes 1376260
  74.7 1.1 %copy-start.2 = (bf16[1792,128]{1,0:T(8,128)(2,1)S(1)}, bf16[1792,128]{1,0:T(8,128)(2,1)}, u32[]{:S(2)}) copy-start(bf16[1792,128]{1,0:T(8,128)(2,1)} %get-tuple-element.11) | copy-start | bytes 1376260

commit v2 on v1

v2 whole, which is shorter than its diff:
```python
import functools
import math

import jax
import jax.numpy as jnp
from jax import lax
from jax.experimental import pallas as pl
from jax.experimental.pallas import tpu as pltpu
from jax.sharding import PartitionSpec as P

SIDE = 32
CELLS = SIDE * SIDE
TILE = 256
MESH = pl.DeviceIdType.MESH
F32 = jnp.float32
BF16 = jnp.bfloat16

plane_offsets = [(-1, -1), (-1, 0), (-1, 1), (0, -1), (0, 0), (0, 1), (1, -1), (1, 0), (1, 1)]
SUM_TYPES = ((F32, F32, F32), (BF16, BF16, BF16))


def kernel(sizes, x_ref, ct_ref, w1_ref, w2_ref, w1t_ref, w2t_ref,
           out_ref, gv_ref, q1_ref, q2_ref,
           xpad, hpad, ctpad, gppad, wide, st_ct, st_gp, pre, gh, back,
           part_out, part_in, back_out, back_in,
           g1, g2, sums1, sums2,
           sx, rx, sxh, rxh, sct, rct, sgh, rgh, sh, rh, shh, rhh, sgp, rgp, sbk, rbk, sred, rred):
    nz, ns, nc, n, planes, shard, piece, norm_scale = sizes
    channels = n * nc
    zi, si, ci = lax.axis_index("samp"), lax.axis_index("slab"), lax.axis_index("chan")
    has_low, has_high = si > 0, si < ns - 1

    barrier = pltpu.get_barrier_semaphore()
    for k in range(1, nc):
        pl.semaphore_signal(barrier, inc=1, device_id={"chan": lax.rem(ci + k, nc)}, device_id_type=MESH)
    for k in range(1, ns):
        pl.semaphore_signal(barrier, inc=1, device_id={"slab": lax.rem(si + k, ns)}, device_id_type=MESH)
    for k in range(1, nz):
        pl.semaphore_signal(barrier, inc=1, device_id={"samp": lax.rem(zi + k, nz)}, device_id_type=MESH)
    pl.semaphore_wait(barrier, nc + ns + nz - 3)

    def rows_of(index):
        return pl.ds(pl.multiple_of(index * n, n), n)

    def send(src, dst, send_sem, recv_sem, axis, index):
        return pltpu.make_async_remote_copy(
            src_ref=src, dst_ref=dst, send_sem=send_sem, recv_sem=recv_sem,
            device_id={axis: index}, device_id_type=MESH)

    def halo_sends(padded, rows, ssem, rsem, slot):
        low = send(padded.at[1, rows], padded.at[planes + 1, rows], ssem.at[2 * slot], rsem.at[2 * slot], "slab", si - 1)
        high = send(padded.at[planes, rows], padded.at[0, rows], ssem.at[2 * slot + 1], rsem.at[2 * slot + 1], "slab", si + 1)
        return low, high

    def start_halo(*args):
        low, high = halo_sends(*args)
        pl.when(has_low)(low.start)
        pl.when(has_high)(high.start)

    def wait_halo(*args):
        low, high = halo_sends(*args)
        pl.when(has_high)(low.wait_recv)
        pl.when(has_low)(high.wait_recv)

    def finish_halo(*args):
        low, high = halo_sends(*args)
        pl.when(has_low)(low.wait_send)
        pl.when(has_high)(high.wait_send)

    own = rows_of(ci)
    everything = pl.ds(0, n)
    inside = pl.ds(1, planes)

    def gather_sends(padded, ssem, rsem):
        return [send(padded.at[1 + d, own], padded.at[1 + d, own], ssem.at[planes * (k - 1) + d],
                     rsem.at[planes * (k - 1) + d], "chan", lax.rem(ci + k, nc))
                for d in range(planes) for k in range(1, nc)]

    def gather_and_forward(padded, ssem, rsem, fsend, frecv):
        for d in range(planes):
            for k in range(1, nc):
                rows = rows_of(lax.rem(ci + nc - k, nc))
                at = planes * (k - 1) + d
                send(padded.at[1 + d, rows], padded.at[1 + d, rows], ssem.at[at], rsem.at[at],
                     "chan", lax.rem(ci + k, nc)).wait_recv()
                low, high = halo_sends(padded, rows, fsend, frecv, k)
                if d == 0:
                    pl.when(has_low)(low.start)
                if d == planes - 1:
                    pl.when(has_high)(high.start)

    def zero_edges(padded):
        @pl.when(jnp.logical_not(has_low))
        def _():
            padded[0] = jnp.zeros(padded.shape[1:], BF16)

        @pl.when(jnp.logical_not(has_high))
        def _():
            padded[planes + 1] = jnp.zeros(padded.shape[1:], BF16)

    cell = lax.broadcasted_iota(jnp.int32, (1, CELLS), 1)
    row, column = cell // SIDE, cell % SIDE
    masks = []
    for b, c in plane_offsets:
        ok = (row + b >= 0) & (row + b < SIDE) & (column + c >= 0) & (column + c < SIDE)
        masks.append(jnp.broadcast_to(jnp.where(ok, 1.0, 0.0).astype(BF16), (16, CELLS)))

    def build(stack, padded, plane, sign=1):
        count = padded.shape[1]

        def body(step, _):
            start = pl.multiple_of(step * 16, 16)
            values = padded[plane, pl.ds(start, 16), :]
            for j, (b, c) in enumerate(plane_offsets):
                shift = (-sign * (SIDE * b + c)) % CELLS
                if shift == 0:
                    moved = values
                else:
                    moved = pltpu.roll(values, shift, 1) * masks[j if sign > 0 else 8 - j]
                stack[plane, pl.ds(pl.multiple_of(j * count + step * 16, 16), 16), :] = moved
            return 0

        lax.fori_loop(0, count // 16, body, 0)

    def convolve(weight, stack, emit, reverse=False):
        def body(step, _):
            cols = pl.ds(pl.multiple_of(step * TILE, TILE), TILE)
            totals = [None] * planes
            for p in range(planes + 2):
                pairs = []
                for d in range(planes):
                    a = d + 2 - p if reverse else p - d
                    if 0 <= a < 3:
                        pairs.append((d, a))
                left = jnp.concatenate([weight[a] for _, a in pairs], axis=0)
                term = jnp.dot(left, stack[p, :, cols], preferred_element_type=F32)
                height = weight.shape[1]
                for at, (d, _) in enumerate(pairs):
                    part = term[at * height : (at + 1) * height]
                    totals[d] = part if totals[d] is None else totals[d] + part
            for d in range(planes):
                emit(d, cols, totals[d])
            return 0

        lax.fori_loop(0, CELLS // TILE, body, 0)

    def filter_grad(total_ref, stack, padded):
        count = stack.shape[1]
        for a in range(3):
            total = None
            for d in range(planes):
                term = lax.dot_general(stack[d + 1], padded[d + a], (((1,), (1,)), ((), ())),
                                       preferred_element_type=F32)
                total = term if total is None else total + term
            total_ref[pl.ds(a * count, count), :] = total
        rest = ns * shard - 3 * count
        if rest:
            total_ref[pl.ds(3 * count, rest), :] = jnp.zeros((rest, channels), F32)

    xpad[inside, own, :] = x_ref[...]
    for copy in gather_sends(xpad, sx, rx):
        copy.start()
    start_halo(xpad, own, sxh, rxh, 0)
    ctpad[inside] = ct_ref[...]
    start_halo(ctpad, everything, sct, rct, 0)

    zero_edges(ctpad)
    zero_edges(xpad)
    for plane in range(1, planes + 1):
        build(st_ct, ctpad, plane, -1)
    wait_halo(ctpad, everything, sct, rct, 0)
    build(st_ct, ctpad, 0, -1)
    build(st_ct, ctpad, planes + 1, -1)

    def reverse_parts(weight_t, stack, sums, outgoing, incoming, ssem, rsem):
        def keep(d, cols, total):
            sums[d, :, cols] = total

        convolve(weight_t, stack, keep, reverse=True)
        for k in range(1, nc):
            target = lax.rem(ci + k, nc)
            outgoing[k - 1] = sums[:, rows_of(target), :].astype(outgoing.dtype)
            send(outgoing.at[k - 1], incoming.at[k - 1], ssem.at[k - 1], rsem.at[k - 1], "chan", target).start()

    def part_copies(outgoing, incoming, ssem, rsem):
        return [send(outgoing.at[k - 1], incoming.at[k - 1], ssem.at[k - 1], rsem.at[k - 1],
                     "chan", lax.rem(ci + k, nc)) for k in range(1, nc)]

    reverse_parts(w2t_ref, st_ct, gh, part_out, part_in, sgh, rgh)

    gather_and_forward(xpad, sx, rx, sxh, rxh)
    for plane in range(1, planes + 1):
        build(wide, xpad, plane)
    for k in range(nc):
        wait_halo(xpad, rows_of(lax.rem(ci + nc - k, nc)), sxh, rxh, k)
    build(wide, xpad, 0)
    build(wide, xpad, planes + 1)

    def hidden_out(d, cols, total):
        pre[d, :, cols] = total
        hpad[d + 1, own, cols] = (total * jax.nn.sigmoid(total)).astype(BF16)

    convolve(w1_ref, wide, hidden_out)
    for copy in gather_sends(hpad, sh, rh):
        copy.start()
    start_halo(hpad, own, shh, rhh, 0)
    zero_edges(hpad)
    zero_edges(gppad)

    for copy in part_copies(part_out, part_in, sgh, rgh):
        copy.wait_recv()

    def slope(step, _):
        d = step // (n // 16)
        rows = pl.ds(pl.multiple_of((step % (n // 16)) * 16, 16), 16)
        total = gh[d, pl.ds(pl.multiple_of(ci * n + (step % (n // 16)) * 16, 16), 16), :]
        for k in range(nc - 1):
            total = total + part_in[k, d, rows, :].astype(F32)
        values = pre[d, rows, :]
        sigma = jax.nn.sigmoid(values)
        gppad[d + 1, rows, :] = (total * (sigma * (1.0 + values * (1.0 - sigma)))).astype(BF16)
        return 0

    lax.fori_loop(0, planes * (n // 16), slope, 0)
    start_halo(gppad, everything, sgp, rgp, 0)
    for plane in range(1, planes + 1):
        build(st_gp, gppad, plane, -1)
    filter_grad(g1, st_gp, xpad)

    nx = ns // 2
    core, xi = lax.rem(si, 2), si // 2
    half = nx * shard

    def span(core_index, x_index=None, samp_index=None):
        begin = core_index * half
        if x_index is None:
            return pl.ds(pl.multiple_of(begin, 16), half)
        begin = begin + x_index * shard
        if samp_index is None:
            return pl.ds(pl.multiple_of(begin, 16), shard)
        return pl.ds(pl.multiple_of(begin + samp_index * piece, 16), piece)

    class Reduction:
        def __init__(self, which, total, buffers, result):
            self.total, self.result = total, result
            self.out1, self.in1, self.out2, self.in2, self.out3, self.in3 = buffers
            self.base = which * 2 * (1 + ns + nz)

        def over_core(self, src, dst, at):
            return send(src, dst, sred.at[self.base + at], rred.at[self.base + at], "slab", 2 * xi + 1 - core)

        def over_x(self, src, dst, k, at):
            return send(src, dst, sred.at[self.base + at], rred.at[self.base + at], "slab",
                        2 * lax.rem(xi + k, nx) + core)

        def over_samp(self, src, dst, k, at):
            return send(src, dst, sred.at[self.base + at], rred.at[self.base + at], "samp", lax.rem(zi + k, nz))

        def core_sum(self):
            return [self.over_core(self.out1, self.in1, 0)]

        def x_sum(self):
            return [self.over_x(self.out2.at[k - 1], self.in2.at[k - 1], k, 1 + k) for k in range(1, nx)]

        def samp_sum(self):
            return [self.over_samp(self.out3.at[k - 1], self.in3.at[k - 1], k, 1 + nx + k) for k in range(1, nz)]

        def samp_gather(self, arriving):
            out = []
            for k in range(1, nz):
                rows = span(core, xi, lax.rem(zi + nz - k, nz) if arriving else zi)
                out.append(self.over_samp(self.result.at[rows], self.result.at[rows], k, 1 + nx + nz + k))
            return out

        def x_gather(self, arriving):
            out = []
            for k in range(1, nx):
                rows = span(core, lax.rem(xi + nx - k, nx) if arriving else xi)
                out.append(self.over_x(self.result.at[rows], self.result.at[rows], k, 1 + nx + 2 * nz + k))
            return out

        def core_gather(self, arriving):
            rows = span(1 - core if arriving else core)
            return [self.over_core(self.result.at[rows], self.result.at[rows], 1)]

        def one(self):
            self.out1[...] = self.total[span(1 - core), :].astype(self.out1.dtype)
            self.core_sum()[0].start()

        def two(self):
            self.core_sum()[0].wait_recv()
            copies = self.x_sum()
            for k in range(nx):
                x_index = lax.rem(xi + k, nx)
                local = pl.ds(pl.multiple_of(x_index * shard, 16), shard)
                summed = self.total[span(core, x_index), :] + self.in1[local, :].astype(F32)
                if k:
                    self.out2[k - 1] = summed.astype(self.out2.dtype)
                    copies[k - 1].start()
                else:
                    self.total[span(core, xi), :] = summed

        def three(self):
            for copy in self.x_sum():
                copy.wait_recv()
            copies = self.samp_sum()
            for k in range(nz):
                samp_index = lax.rem(zi + k, nz)
                rows = span(core, xi, samp_index)
                summed = self.total[rows, :]
                for m in range(nx - 1):
                    summed = summed + self.in2[m, pl.ds(pl.multiple_of(samp_index * piece, 16), piece), :].astype(F32)
                if k:
                    self.out3[k - 1] = summed.astype(self.out3.dtype)
                    copies[k - 1].start()
                else:
                    self.total[rows, :] = summed

        def four(self):
            for copy in self.samp_sum():
                copy.wait_recv()
            rows = span(core, xi, zi)
            summed = self.total[rows, :]
            for k in range(nz - 1):
                summed = summed + self.in3[k].astype(F32)
            self.result[rows, :] = (summed * norm_scale).astype(BF16)
            for copy in self.samp_gather(False):
                copy.start()

        def five(self):
            for copy in self.samp_gather(True):
                copy.wait_recv()
            for copy in self.x_gather(False):
                copy.start()

        def six(self):
            for copy in self.x_gather(True):
                copy.wait_recv()
            self.core_gather(False)[0].start()

        def seven(self):
            self.core_gather(True)[0].wait_recv()

        def finish(self):
            for copy in (self.core_sum() + self.x_sum() + self.samp_sum() + self.samp_gather(False)
                         + self.x_gather(False) + self.core_gather(False)):
                copy.wait_send()

    first = Reduction(0, g1, sums1, q1_ref)
    second = Reduction(1, g2, sums2, q2_ref)
    first.one()

    wait_halo(gppad, everything, sgp, rgp, 0)
    build(st_gp, gppad, 0, -1)
    build(st_gp, gppad, planes + 1, -1)
    reverse_parts(w1t_ref, st_gp, back, back_out, back_in, sbk, rbk)

    first.two()
    gather_and_forward(hpad, sh, rh, shh, rhh)
    for k in range(nc):
        wait_halo(hpad, rows_of(lax.rem(ci + nc - k, nc)), shh, rhh, k)
    filter_grad(g2, st_ct, hpad)
    second.one()
    first.three()
    for plane in range(planes):
        build(wide, hpad, plane)
    second.two()
    for plane in range(planes, planes + 2):
        build(wide, hpad, plane)

    def block(d, cols, total):
        out_ref[d, :, cols] = (x_ref[d, :, cols].astype(F32) + total).astype(BF16)

    first.four()
    convolve(w2_ref, wide, block)
    second.three()
    first.five()

    for copy in part_copies(back_out, back_in, sbk, rbk):
        copy.wait_recv()

    def volume_grad(step, _):
        d = step // (n // 16)
        rows = pl.ds(pl.multiple_of((step % (n // 16)) * 16, 16), 16)
        total = back[d, pl.ds(pl.multiple_of(ci * n + (step % (n // 16)) * 16, 16), 16), :]
        for k in range(nc - 1):
            total = total + back_in[k, d, rows, :].astype(F32)
        gv_ref[d, rows, :] = (ct_ref[d, rows, :].astype(F32) + total).astype(BF16)
        return 0

    lax.fori_loop(0, planes * (n // 16), volume_grad, 0)
    second.four()
    first.six()
    second.five()
    second.six()
    first.seven()
    second.seven()

    for copy in gather_sends(xpad, sx, rx) + gather_sends(hpad, sh, rh):
        copy.wait_send()
    for copy in part_copies(part_out, part_in, sgh, rgh) + part_copies(back_out, back_in, sbk, rbk):
        copy.wait_send()
    for k in range(nc):
        rows = rows_of(lax.rem(ci + nc - k, nc))
        finish_halo(xpad, rows, sxh, rxh, k)
        finish_halo(hpad, rows, shh, rhh, k)
    finish_halo(ctpad, everything, sct, rct, 0)
    finish_halo(gppad, everything, sgp, rgp, 0)
    first.finish()
    second.finish()


def per_device(volume, cotangent, filter_one, filter_two):
    n, planes, cells = volume.shape[1:]
    nz, ns, nc = (lax.axis_size(axis) for axis in ("samp", "slab", "chan"))
    channels = n * nc
    norm_scale = 1.0 / math.sqrt(nz * planes * ns * cells)
    unit = 16 * ns * nz
    rows = -(-27 * n // unit) * unit
    shard, piece = rows // ns, rows // ns // nz

    def forward(weight):
        return jnp.transpose(weight.reshape(n, 3, 9 * channels), (1, 0, 2))

    def backward(weight):
        return jnp.transpose(weight.reshape(n, 3, 9, channels), (1, 3, 2, 0)).reshape(3, channels, 9 * n)

    x = jnp.transpose(volume[0], (1, 0, 2))
    ct = jnp.transpose(cotangent[0], (1, 0, 2))
    vmem = pl.BlockSpec(memory_space=pltpu.VMEM)
    padded = planes + 2
    dma = pltpu.SemaphoreType.DMA

    nx = ns // 2

    def reduction_buffers(dtypes):
        one, two, three = dtypes
        return [pltpu.VMEM((nx * shard, channels), one)] * 2 + [
            pltpu.VMEM((nx - 1, shard, channels), two)] * 2 + [
            pltpu.VMEM((nz - 1, piece, channels), three)] * 2

    scratch = [
        pltpu.VMEM((padded, channels, cells), BF16),
        pltpu.VMEM((padded, channels, cells), BF16),
        pltpu.VMEM((padded, n, cells), BF16),
        pltpu.VMEM((padded, n, cells), BF16),
        pltpu.VMEM((padded, 9 * channels, cells), BF16),
        pltpu.VMEM((padded, 9 * n, cells), BF16),
        pltpu.VMEM((padded, 9 * n, cells), BF16),
        pltpu.VMEM((planes, n, cells), F32),
        pltpu.VMEM((planes, channels, cells), F32),
        pltpu.VMEM((planes, channels, cells), F32),
    ] + [pltpu.VMEM((nc - 1, planes, n, cells), BF16)] * 4 + [
        pltpu.VMEM((rows, channels), F32),
        pltpu.VMEM((rows, channels), F32),
        reduction_buffers(SUM_TYPES[0]),
        reduction_buffers(SUM_TYPES[1]),
        dma((planes * nc,)), dma((planes * nc,)), dma((2 * nc,)), dma((2 * nc,)),
        dma((2,)), dma((2,)), dma((nc,)), dma((nc,)),
        dma((planes * nc,)), dma((planes * nc,)), dma((2 * nc,)), dma((2 * nc,)),
        dma((2,)), dma((2,)), dma((nc,)), dma((nc,)),
        dma((4 * (1 + ns + nz),)), dma((4 * (1 + ns + nz),)),
    ]
    sizes = (nz, ns, nc, n, planes, shard, piece, norm_scale)
    block, grad_volume, one, two = pl.pallas_call(
        functools.partial(kernel, sizes),
        out_shape=(
            jax.ShapeDtypeStruct((planes, n, cells), BF16),
            jax.ShapeDtypeStruct((planes, n, cells), BF16),
            jax.ShapeDtypeStruct((rows, channels), BF16),
            jax.ShapeDtypeStruct((rows, channels), BF16),
        ),
        in_specs=[vmem] * 6,
        out_specs=(vmem,) * 4,
        scratch_shapes=scratch,
        compiler_params=pltpu.CompilerParams(
            collective_id=0, has_side_effects=True, vmem_limit_bytes=56 * 1024 * 1024),
        cost_estimate=pl.CostEstimate(
            flops=6 * 2 * planes * cells * n * 27 * channels, bytes_accessed=8 << 20, transcendentals=planes * n * cells),
        name="residual_pair",
    )(x, ct, forward(filter_one), forward(filter_two), backward(filter_one), backward(filter_two))

    def filter_out(values):
        values = values[: 27 * n].reshape(3, 9, n, channels)
        return jnp.transpose(values, (2, 0, 1, 3)).reshape(n, 27, channels).astype(F32)

    return (
        jnp.transpose(block, (1, 0, 2))[None],
        jnp.transpose(grad_volume, (1, 0, 2))[None],
        filter_out(one),
        filter_out(two),
    )


def solution(mesh):
    return jax.shard_map(
        per_device,
        mesh=mesh,
        in_specs=(
            P("samp", "chan", "slab", None),
            P("samp", "chan", "slab", None),
            P("chan", None, None),
            P("chan", None, None),
        ),
        out_specs=(
            P("samp", "chan", "slab", None),
            P("samp", "chan", "slab", None),
            P("chan", None, None),
            P("chan", None, None),
        ),
        check_vma=False,
    )
```

time: 77.7 us -> 74.8 us (0.963)
  Pallas kernels: 64.9 us -> 61.8 us
    pallas_call x1, Pallas kernels: 64.9 us -> 61.8 us  [per_device(): pl.pallas_call(functools.partial(kernel, sizes), out_shape=(jax.ShapeDtyp...]
    rev x2 -> x0, local copies, waits for them, and re-layouts: 1.07 us -> none  [backward(): flipped = weight[:, ::-1, :].reshape(n, 3, 9, channels)]
    reshape x2, local copies, waits for them, and re-layouts: 1.99 us -> 3.04 us  [backward(): jnp.transpose(weight.reshape(n, 3, 9, channels), (1, 3, 2, 0))]
where the time goes in v2:
time: 74.8 us; the launch traced here: 74.5 us
  Pallas kernels  61.8 us (83%)
  local copies, waits for them, and re-layouts  9.95 us (13%)
  other arithmetic  2.02 us (3%)
    pallas_call x1, Pallas kernels, per_device(): pl.pallas_call(functools.partial(kernel, sizes), out_shape=(jax.ShapeDtyp...  61.8 us
    unnamed x18, local copies, waits for them, and re-layouts  4.41 us
    reshape x2, local copies, waits for them, and re-layouts, backward(): jnp.transpose(weight.reshape(n, 3, 9, channels), (1, 3, 2, 0))  3.04 us
    convert_element_type x2, other arithmetic, filter_out(): jnp.transpose(values, (2, 0, 1, 3)).reshape(n, 27, channels).astype(F32)  2.02 us

profile of v2, /device:TPU:0, one launch (start us, length us, event | category | flops | bytes accessed | tf_op | source)
XLA Modules:
  0.0 74.5 jit_solution(14308217228058857886)
XLA Ops:
  0.6 0.0 copy-start
  0.6 2.1 %copy.21.w2t_ref = bf16[3,128,576]{2,1,0:T(8,128)(2,1)} copy(bf16[3,128,576]{1,2,0:T(8,128)(2,1)} %bitcast.39) | data formatting | bytes 884736 | tf_op jit(solution)/shard_map/reshape | solution.py:426
  2.7 0.0 copy-done
  2.7 1.0 %copy.20.w1t_ref = bf16[3,128,576]{2,1,0:T(8,128)(2,1)} copy(bf16[3,128,576]{1,2,0:T(8,128)(2,1)S(1)} %bitcast.38) | data formatting | bytes 884736 | tf_op jit(solution)/shard_map/reshape | solution.py:426
  3.7 0.3 copy.16
  4.0 0.0 copy-start.1
  4.0 0.2 reshape.38
  4.2 0.8 %copy-done.1 = bf16[64,27,128]{2,0,1:T(8,128)(2,1)S(1)} copy-done((bf16[64,27,128]{2,0,1:T(8,128)(2,1)S(1)}, bf16[64,27,128]{2,0,1:T(8,128)(2,1)}, u32[]{:S(2)}) %copy-start.1) | copy-done | bytes 442392
  5.0 0.3 copy.18
  5.3 0.2 reshape.39
  5.5 0.0 copy-start.5
  5.5 0.0 copy-start.6
  5.6 1.1 %copy_bitcast_fusion = (bf16[3,64,1152]{2,1,0:T(8,128)(2,1)}, bf16[3,64,1152]{2,1,0:T(8,128)(2,1)}) fusion(bf16[64,3,1152]{2,1,0:T(4,128)(2,1)S(1)} %reshape.39, bf16[64,3,1152]{2,1,0:T(4,128)(2,1)S(1)} %reshape.38), kind=kLoop, calls=%fused_computation | loop fusion | bytes 1769472 | tf_op jit(solution)/shard_map/transpose | solution.py:423
  6.6 0.0 copy-done.5
  6.6 0.0 copy-done.6
  6.6 0.9 %copy_bitcast_fusion.2 = (bf16[2,64,1024]{2,1,0:T(8,128)(2,1)}, bf16[2,64,1024]{2,1,0:T(8,128)(2,1)}) fusion(bf16[1,64,2,1024]{3,2,1,0:T(2,128)(2,1)S(1)} %copy-done.5, bf16[1,64,2,1024]{3,2,1,0:T(2,128)(2,1)S(1)} %copy-done.6), kind=kLoop, calls=%fused_computation.2 | loop fusion | bytes 1048576 | tf_op jit(solution)/shard_map/transpose | solution.py:429
  7.5 61.8 %residual_pair.1 = (bf16[2,64,1024]{2,1,0:T(8,128)(2,1)}, bf16[2,64,1024]{2,1,0:T(8,128)(2,1)}, bf16[1792,128]{1,0:T(8,128)(2,1)}, bf16[1792,128]{1,0:T(8,128)(2,1)}) custom-call(bf16[2,64,1024]{2,1,0:T(8,128)(2,1)} %get-tuple-element.23.x_ref, bf16[2,64,1024]{2,1,0:T(8,128)(2,1)} %get-tuple-element.22.ct_ref, ...), custom_call_target="tpu_custom_call" | custom-call | flops 5435817984 | bytes 8388608 | tf_op jit(solution)/shard_map/residual_pair/pallas_call | solution.py:465
  69.4 0.0 copy-start.4
  69.4 0.0 copy-start.3
  69.4 2.0 %copy.22 = bf16[1,64,2,1024]{3,2,1,0:T(2,128)(2,1)} copy(bf16[1,64,2,1024]{3,1,2,0:T(8,128)(2,1)} %bitcast.45) | data formatting | bytes 524288
  71.4 0.0 copy-done.4
  71.4 1.0 %copy.23 = bf16[1,64,2,1024]{3,2,1,0:T(2,128)(2,1)} copy(bf16[1,64,2,1024]{3,1,2,0:T(8,128)(2,1)S(1)} %bitcast.44) | data formatting | bytes 524288
  72.3 0.0 copy-done.3
  72.4 0.0 copy-start.2
  72.4 1.0 %convert.6 = f32[3,9,64,128]{3,2,1,0:T(8,128)} convert(bf16[3,9,64,128]{3,2,1,0:T(8,128)(2,1)S(1)} %bitcast.40) | non-fusion elementwise | flops 221184 | bytes 1327104 | tf_op jit(solution)/shard_map/convert_element_type | solution.py:485
  73.4 0.0 copy-done.2
  73.5 1.0 %convert.7 = f32[3,9,64,128]{3,2,1,0:T(8,128)} convert(bf16[3,9,64,128]{3,2,1,0:T(8,128)(2,1)S(1)} %bitcast.41) | non-fusion elementwise | flops 221184 | bytes 1327104 | tf_op jit(solution)/shard_map/convert_element_type | solution.py:485
  (2 shorter events, 0.1 us)
Async XLA Ops:
  0.6 2.1 %copy-start = (bf16[64,27,128]{2,0,1:T(8,128)(2,1)S(1)}, bf16[64,27,128]{2,0,1:T(8,128)(2,1)}, u32[]{:S(2)}) copy-start(bf16[64,27,128]{2,0,1:T(8,128)(2,1)} %param.6) | copy-start | bytes 1327108
  4.0 1.0 %copy-start.1 = (bf16[64,27,128]{2,0,1:T(8,128)(2,1)S(1)}, bf16[64,27,128]{2,0,1:T(8,128)(2,1)}, u32[]{:S(2)}) copy-start(bf16[64,27,128]{2,0,1:T(8,128)(2,1)} %param.7) | copy-start | bytes 1327108
  5.5 1.1 %copy-start.5 = (bf16[1,64,2,1024]{3,2,1,0:T(2,128)(2,1)S(1)}, bf16[1,64,2,1024]{3,2,1,0:T(2,128)(2,1)}, u32[]{:S(2)}) copy-start(bf16[1,64,2,1024]{3,2,1,0:T(2,128)(2,1)} %param.5) | copy-start | bytes 786436
  5.5 1.1 %copy-start.6 = (bf16[1,64,2,1024]{3,2,1,0:T(2,128)(2,1)S(1)}, bf16[1,64,2,1024]{3,2,1,0:T(2,128)(2,1)}, u32[]{:S(2)}) copy-start(bf16[1,64,2,1024]{3,2,1,0:T(2,128)(2,1)} %param.4) | copy-start | bytes 786436
  69.4 2.0 %copy-start.4 = (bf16[2,64,1024]{2,1,0:T(8,128)(2,1)S(1)}, bf16[2,64,1024]{2,1,0:T(8,128)(2,1)}, u32[]{:S(2)}) copy-start(bf16[2,64,1024]{2,1,0:T(8,128)(2,1)} %get-tuple-element.9) | copy-start | bytes 786436
  69.4 3.0 %copy-start.3 = (bf16[1792,128]{1,0:T(8,128)(2,1)S(1)}, bf16[1792,128]{1,0:T(8,128)(2,1)}, u32[]{:S(2)}) copy-start(bf16[1792,128]{1,0:T(8,128)(2,1)} %get-tuple-element.10) | copy-start | bytes 1376260
  72.4 1.1 %copy-start.2 = (bf16[1792,128]{1,0:T(8,128)(2,1)S(1)}, bf16[1792,128]{1,0:T(8,128)(2,1)}, u32[]{:S(2)}) copy-start(bf16[1792,128]{1,0:T(8,128)(2,1)} %get-tuple-element.11) | copy-start | bytes 1376260

commit v3 on v2

--- a/solution.py
+++ b/solution.py
@@ -10,6 +10,9 @@
 
 SIDE = 32
 CELLS = SIDE * SIDE
+LANES = 128
+GROUPS = LANES // SIDE
+BLOCKS = CELLS // LANES
 TILE = 256
 MESH = pl.DeviceIdType.MESH
 F32 = jnp.float32
@@ -19,9 +22,9 @@
 SUM_TYPES = ((F32, F32, F32), (BF16, BF16, BF16))
 
 
-def kernel(sizes, x_ref, ct_ref, w1_ref, w2_ref, w1t_ref, w2t_ref,
+def kernel(sizes, x_ref, ct_ref, w1_ref, w2_ref,
            out_ref, gv_ref, q1_ref, q2_ref,
-           xpad, hpad, ctpad, gppad, wide, st_ct, st_gp, pre, gh, back,
+           fw1, fw2, bw1, bw2, result, xpad, hpad, ctpad, gppad, wide, st_ct, st_gp, pre, gh, back,
            part_out, part_in, back_out, back_in,
            g1, g2, sums1, sums2,
            sx, rx, sxh, rxh, sct, rct, sgh, rgh, sh, rh, shh, rhh, sgp, rgp, sbk, rbk, sred, rred):
@@ -98,29 +101,82 @@
         def _():
             padded[planes + 1] = jnp.zeros(padded.shape[1:], BF16)
 
-    cell = lax.broadcasted_iota(jnp.int32, (1, CELLS), 1)
-    row, column = cell // SIDE, cell % SIDE
-    masks = []
-    for b, c in plane_offsets:
-        ok = (row + b >= 0) & (row + b < SIDE) & (column + c >= 0) & (column + c < SIDE)
-        masks.append(jnp.broadcast_to(jnp.where(ok, 1.0, 0.0).astype(BF16), (16, CELLS)))
+    lane = lax.broadcasted_iota(jnp.int32, (1, LANES), 1)
+    group, column = lane // SIDE, lane % SIDE
+
+    def mask_of(ok):
+        return jnp.where(ok, 1.0, 0.0).astype(BF16)
+
+    def kept(group_step, c):
+        return mask_of((group + group_step >= 0) & (group + group_step < GROUPS)
+                       & (column + c >= 0) & (column + c < SIDE))
+
+    group_masks = [mask_of(group == g) for g in range(GROUPS)]
+    shift_masks = {(step, c): kept(step, c) for step in (-1, 0, 1) for c in (-1, 0, 1)}
+
+    def lane_block(values, t):
+        return values[:, t * LANES : (t + 1) * LANES]
+
+    def turned(values, shift):
+        return values if shift % LANES == 0 else pltpu.roll(values, shift % LANES, 1)
+
+    def to_blocks(values):
+        out = []
+        for t in range(BLOCKS):
+            total = None
+            for g in range(GROUPS):
+                row = BLOCKS * g + t
+                term = turned(lane_block(values, row // GROUPS), SIDE * (g - row % GROUPS)) * group_masks[g]
+                total = term if total is None else total + term
+            out.append(total)
+        return jnp.concatenate(out, axis=1)
+
+    def from_blocks(values):
+        out = []
+        for m in range(BLOCKS):
+            total = None
+            for g in range(GROUPS):
+                row = GROUPS * m + g
+                term = turned(lane_block(values, row % BLOCKS), SIDE * (g - row // BLOCKS)) * group_masks[g]
+                total = term if total is None else total + term
+            out.append(total)
+        return jnp.concatenate(out, axis=1)
 
     def build(stack, padded, plane, sign=1):
         count = padded.shape[1]
+        height = min(32, count)
 
         def body(step, _):
-            start = pl.multiple_of(step * 16, 16)
-            values = padded[plane, pl.ds(start, 16), :]
+            values = padded[plane, pl.ds(pl.multiple_of(step * height, 16), height), :]
+            sources = [lane_block(values, t) for t in range(BLOCKS)]
+            moved = {}
+            for c in (-1, 0, 1):
+                for t in range(BLOCKS):
+                    moved[t, 0, c] = turned(sources[t], -c) * shift_masks[0, c] if c else sources[t]
+                moved[0, 1, c] = turned(sources[0], -SIDE - c) * shift_masks[1, c]
+                moved[BLOCKS - 1, -1, c] = turned(sources[BLOCKS - 1], SIDE - c) * shift_masks[-1, c]
             for j, (b, c) in enumerate(plane_offsets):
-                shift = (-sign * (SIDE * b + c)) % CELLS
-                if shift == 0:
-                    moved = values
-                else:
-                    moved = pltpu.roll(values, shift, 1) * masks[j if sign > 0 else 8 - j]
-                stack[plane, pl.ds(pl.multiple_of(j * count + step * 16, 16), 16), :] = moved
+                b, c = sign * b, sign * c
+                for t in range(BLOCKS):
+                    source = t + b
+                    wrap = 1 if source == BLOCKS else -1 if source < 0 else 0
+                    stack[plane, pl.ds(pl.multiple_of(j * count + step * height, 16), height),
+                          t * LANES : (t + 1) * LANES] = moved[source % BLOCKS, wrap, c]
             return 0
 
-        lax.fori_loop(0, count // 16, body, 0)
+        lax.fori_loop(0, count // height, body, 0)
+
+    def lay_forward(target, weight):
+        for tap in range(27):
+            target[tap // 9, :, (tap % 9) * channels : (tap % 9 + 1) * channels] = weight[tap]
+
+    def lay_backward(target, weight):
+        group_size = max(1, LANES // n)
+        for a in range(3):
+            for j in range(0, 9, group_size):
+                taps = min(group_size, 9 - j)
+                piece_of = weight[pl.ds(9 * a + j, taps)].reshape(taps * n, channels)
+                target[a, :, j * n : (j + taps) * n] = piece_of.T
 
     def convolve(weight, stack, emit, reverse=False):
         def body(step, _):
@@ -157,13 +213,16 @@
         if rest:
             total_ref[pl.ds(3 * count, rest), :] = jnp.zeros((rest, channels), F32)
 
-    xpad[inside, own, :] = x_ref[...]
+    for d in range(planes):
+        xpad[1 + d, own, :] = to_blocks(x_ref[d])
     for copy in gather_sends(xpad, sx, rx):
         copy.start()
     start_halo(xpad, own, sxh, rxh, 0)
-    ctpad[inside] = ct_ref[...]
+    for d in range(planes):
+        ctpad[1 + d] = to_blocks(ct_ref[d])
     start_halo(ctpad, everything, sct, rct, 0)
 
+    lay_backward(bw2, w2_ref)
     zero_edges(ctpad)
     zero_edges(xpad)
     for plane in range(1, planes + 1):
@@ -186,8 +245,9 @@
         return [send(outgoing.at[k - 1], incoming.at[k - 1], ssem.at[k - 1], rsem.at[k - 1],
                      "chan", lax.rem(ci + k, nc)) for k in range(1, nc)]
 
-    reverse_parts(w2t_ref, st_ct, gh, part_out, part_in, sgh, rgh)
-
+    reverse_parts(bw2, st_ct, gh, part_out, part_in, sgh, rgh)
+
+    lay_forward(fw1, w1_ref)
     gather_and_forward(xpad, sx, rx, sxh, rxh)
     for plane in range(1, planes + 1):
         build(wide, xpad, plane)
@@ -200,11 +260,13 @@
         pre[d, :, cols] = total
         hpad[d + 1, own, cols] = (total * jax.nn.sigmoid(total)).astype(BF16)
 
-    convolve(w1_ref, wide, hidden_out)
+    convolve(fw1, wide, hidden_out)
     for copy in gather_sends(hpad, sh, rh):
         copy.start()
     start_halo(hpad, own, shh, rhh, 0)
     zero_edges(hpad)
+    lay_backward(bw1, w1_ref)
+    lay_forward(fw2, w2_ref)
     zero_edges(gppad)
 
     for copy in part_copies(part_out, part_in, sgh, rgh):
@@ -353,7 +415,7 @@
     wait_halo(gppad, everything, sgp, rgp, 0)
     build(st_gp, gppad, 0, -1)
     build(st_gp, gppad, planes + 1, -1)
-    reverse_parts(w1t_ref, st_gp, back, back_out, back_in, sbk, rbk)
+    reverse_parts(bw1, st_gp, back, back_out, back_in, sbk, rbk)
 
     first.two()
     gather_and_forward(hpad, sh, rh, shh, rhh)
@@ -369,12 +431,14 @@
         build(wide, hpad, plane)
 
     def block(d, cols, total):
-        out_ref[d, :, cols] = (x_ref[d, :, cols].astype(F32) + total).astype(BF16)
+        result[d, :, cols] = (xpad[1 + d, own, cols].astype(F32) + total).astype(BF16)
 
     first.four()
-    convolve(w2_ref, wide, block)
+    convolve(fw2, wide, block)
     second.three()
     first.five()
+    for d in range(planes):
+        out_ref[d] = from_blocks(result[d])
 
     for copy in part_copies(back_out, back_in, sbk, rbk):
         copy.wait_recv()
@@ -385,7 +449,7 @@
         total = back[d, pl.ds(pl.multiple_of(ci * n + (step % (n // 16)) * 16, 16), 16), :]
         for k in range(nc - 1):
             total = total + back_in[k, d, rows, :].astype(F32)
-        gv_ref[d, rows, :] = (ct_ref[d, rows, :].astype(F32) + total).astype(BF16)
+        gv_ref[d, rows, :] = from_blocks((ctpad[d + 1, rows, :].astype(F32) + total).astype(BF16))
         return 0
 
     lax.fori_loop(0, planes * (n // 16), volume_grad, 0)
@@ -419,11 +483,8 @@
     rows = -(-27 * n // unit) * unit
     shard, piece = rows // ns, rows // ns // nz
 
-    def forward(weight):
-        return jnp.transpose(weight.reshape(n, 3, 9 * channels), (1, 0, 2))
-
-    def backward(weight):
-        return jnp.transpose(weight.reshape(n, 3, 9, channels), (1, 3, 2, 0)).reshape(3, channels, 9 * n)
+    def by_tap(weight):
+        return jnp.transpose(weight, (1, 0, 2))
 
     x = jnp.transpose(volume[0], (1, 0, 2))
     ct = jnp.transpose(cotangent[0], (1, 0, 2))
@@ -439,7 +500,8 @@
             pltpu.VMEM((nx - 1, shard, channels), two)] * 2 + [
             pltpu.VMEM((nz - 1, piece, channels), three)] * 2
 
-    scratch = [
+    scratch = [pltpu.VMEM((3, n, 9 * channels), BF16)] * 2 + [pltpu.VMEM((3, channels, 9 * n), BF16)] * 2 + [
+        pltpu.VMEM((planes, n, cells), BF16),
         pltpu.VMEM((padded, channels, cells), BF16),
         pltpu.VMEM((padded, channels, cells), BF16),
         pltpu.VMEM((padded, n, cells), BF16),
@@ -470,7 +532,7 @@
             jax.ShapeDtypeStruct((rows, channels), BF16),
             jax.ShapeDtypeStruct((rows, channels), BF16),
         ),
-        in_specs=[vmem] * 6,
+        in_specs=[vmem] * 4,
         out_specs=(vmem,) * 4,
         scratch_shapes=scratch,
         compiler_params=pltpu.CompilerParams(
@@ -478,7 +540,7 @@
         cost_estimate=pl.CostEstimate(
             flops=6 * 2 * planes * cells * n * 27 * channels, bytes_accessed=8 << 20, transcendentals=planes * n * cells),
         name="residual_pair",
-    )(x, ct, forward(filter_one), forward(filter_two), backward(filter_one), backward(filter_two))
+    )(x, ct, by_tap(filter_one), by_tap(filter_two))
 
     def filter_out(values):
         values = values[: 27 * n].reshape(3, 9, n, channels)

time: 74.8 us -> 68.2 us (0.912)
  local copies, waits for them, and re-layouts: 9.95 us -> 5.02 us
  Pallas kernels: 61.8 us -> 60.3 us
    reshape x4 -> x0, local copies, waits for them, and re-layouts: 3.49 us -> none  [the longest x2 3.04 us: backward(): jnp.transpose(weight.reshape(n, 3, 9, channels), (1, 3, 2, 0))]
    pallas_call x1, Pallas kernels: 61.8 us -> 60.3 us  [per_device(): pl.pallas_call(functools.partial(kernel, sizes), out_shape=(jax.ShapeDtyp...]
    unnamed x18 -> x8, local copies, waits for them, and re-layouts: 4.41 us -> 3.02 us
    transpose x1 -> x0, local copies, waits for them, and re-layouts: 1.07 us -> none  [forward(): return jnp.transpose(weight.reshape(n, 3, 9 * channels), (1, 0, 2))]
    transpose x1, local copies, waits for them, and re-layouts: 0.91 us -> 1.94 us  [per_device(): ct = jnp.transpose(cotangent[0], (1, 0, 2))]
where the time goes in v3:
time: 68.2 us; the launch traced here: 68 us
  Pallas kernels  60.3 us (88%)
  local copies, waits for them, and re-layouts  5.02 us (7%)
  other arithmetic  2.02 us (3%)
    pallas_call x1, Pallas kernels, per_device(): pl.pallas_call(functools.partial(kernel, sizes), out_shape=(jax.ShapeDtyp...  60.3 us
    unnamed x8, local copies, waits for them, and re-layouts  3.02 us
    convert_element_type x2, other arithmetic, filter_out(): jnp.transpose(values, (2, 0, 1, 3)).reshape(n, 27, channels).astype(F32)  2.02 us
    transpose x1, local copies, waits for them, and re-layouts, per_device(): ct = jnp.transpose(cotangent[0], (1, 0, 2))  1.94 us

profile of v3, /device:TPU:0, one launch (start us, length us, event | category | flops | bytes accessed | tf_op | source)
XLA Modules:
  0.0 68.0 jit_solution(17800738314130486941)
XLA Ops:
  0.6 1.9 %copy_bitcast_fusion = (bf16[2,64,1024]{2,1,0:T(8,128)(2,1)}, bf16[2,64,1024]{2,1,0:T(8,128)(2,1)}) fusion(bf16[1,64,2,1024]{3,2,1,0:T(2,128)(2,1)} %param.5, bf16[1,64,2,1024]{3,2,1,0:T(2,128)(2,1)} %param.4), kind=kLoop, calls=%fused_computation | loop fusion | bytes 1048576 | tf_op jit(solution)/shard_map/transpose | solution.py:490
  2.6 60.3 %residual_pair.1 = (bf16[2,64,1024]{2,1,0:T(8,128)(2,1)}, bf16[2,64,1024]{2,1,0:T(8,128)(2,1)}, bf16[1792,128]{1,0:T(8,128)(2,1)}, bf16[1792,128]{1,0:T(8,128)(2,1)}) custom-call(bf16[2,64,1024]{2,1,0:T(8,128)(2,1)} %get-tuple-element.17.x_ref, bf16[2,64,1024]{2,1,0:T(8,128)(2,1)} %get-tuple-element.16.ct_ref, bf16[27,64,128]{2,1,0:T(8,128)(2,1)} %bitcast.32, ...), custom_call_target="tpu_custom_call" | custom-call | flops 5435817984 | bytes 8388608 | tf_op jit(solution)/shard_map/residual_pair/pallas_call | solution.py:527
  62.9 0.0 copy-start.2
  62.9 0.0 copy-start.1
  62.9 2.0 %copy.10 = bf16[1,64,2,1024]{3,2,1,0:T(2,128)(2,1)} copy(bf16[1,64,2,1024]{3,1,2,0:T(8,128)(2,1)} %bitcast.31) | data formatting | bytes 524288
  64.9 0.0 copy-done.2
  64.9 1.0 %copy.11 = bf16[1,64,2,1024]{3,2,1,0:T(2,128)(2,1)} copy(bf16[1,64,2,1024]{3,1,2,0:T(8,128)(2,1)S(1)} %bitcast.30) | data formatting | bytes 524288
  65.8 0.0 copy-done.1
  65.9 0.0 copy-start
  65.9 1.0 %convert.6 = f32[3,9,64,128]{3,2,1,0:T(8,128)} convert(bf16[3,9,64,128]{3,2,1,0:T(8,128)(2,1)S(1)} %bitcast.26) | non-fusion elementwise | flops 221184 | bytes 1327104 | tf_op jit(solution)/shard_map/convert_element_type | solution.py:547
  66.9 0.0 copy-done
  67.0 1.0 %convert.7 = f32[3,9,64,128]{3,2,1,0:T(8,128)} convert(bf16[3,9,64,128]{3,2,1,0:T(8,128)(2,1)S(1)} %bitcast.27) | non-fusion elementwise | flops 221184 | bytes 1327104 | tf_op jit(solution)/shard_map/convert_element_type | solution.py:547
  (2 shorter events, 0.1 us)
Async XLA Ops:
  62.9 2.0 %copy-start.2 = (bf16[2,64,1024]{2,1,0:T(8,128)(2,1)S(1)}, bf16[2,64,1024]{2,1,0:T(8,128)(2,1)}, u32[]{:S(2)}) copy-start(bf16[2,64,1024]{2,1,0:T(8,128)(2,1)} %get-tuple-element.9) | copy-start | bytes 786436
  62.9 3.0 %copy-start.1 = (bf16[1792,128]{1,0:T(8,128)(2,1)S(1)}, bf16[1792,128]{1,0:T(8,128)(2,1)}, u32[]{:S(2)}) copy-start(bf16[1792,128]{1,0:T(8,128)(2,1)} %get-tuple-element.10) | copy-start | bytes 1376260
  65.9 1.1 %copy-start = (bf16[1792,128]{1,0:T(8,128)(2,1)S(1)}, bf16[1792,128]{1,0:T(8,128)(2,1)}, u32[]{:S(2)}) copy-start(bf16[1792,128]{1,0:T(8,128)(2,1)} %get-tuple-element.11) | copy-start | bytes 1376260

commit v4 on v3

--- a/solution.py
+++ b/solution.py
@@ -19,15 +19,14 @@
 BF16 = jnp.bfloat16
 
 plane_offsets = [(-1, -1), (-1, 0), (-1, 1), (0, -1), (0, 0), (0, 1), (1, -1), (1, 0), (1, 1)]
-SUM_TYPES = ((F32, F32, F32), (BF16, BF16, BF16))
+SUM_TYPES = ((BF16, BF16, BF16), (BF16, BF16, BF16))
 
 
 def kernel(sizes, x_ref, ct_ref, w1_ref, w2_ref,
            out_ref, gv_ref, q1_ref, q2_ref,
-           fw1, fw2, bw1, bw2, result, xpad, hpad, ctpad, gppad, wide, st_ct, st_gp, pre, gh, back,
-           part_out, part_in, back_out, back_in,
+           fw1, fw2, bw1, bw2, wall1, wall2, result, xpad, hpad, ctpad, gppad, wide, st_ct, st_gp, pre,
            g1, g2, sums1, sums2,
-           sx, rx, sxh, rxh, sct, rct, sgh, rgh, sh, rh, shh, rhh, sgp, rgp, sbk, rbk, sred, rred):
+           sx, rx, sxh, rxh, sct, rct, scth, rcth, shh, rhh, sgp, rgp, sw, rw, sred, rred):
     nz, ns, nc, n, planes, shard, piece, norm_scale = sizes
     channels = n * nc
     zi, si, ci = lax.axis_index("samp"), lax.axis_index("slab"), lax.axis_index("chan")
@@ -71,7 +70,7 @@
         pl.when(has_high)(high.wait_send)
 
     own = rows_of(ci)
-    everything = pl.ds(0, n)
+    everything = pl.ds(0, channels)
     inside = pl.ds(1, planes)
 
     def gather_sends(padded, ssem, rsem):
@@ -168,17 +167,16 @@
 
     def lay_forward(target, weight):
         for tap in range(27):
-            target[tap // 9, :, (tap % 9) * channels : (tap % 9 + 1) * channels] = weight[tap]
+            target[tap // 9, :, (tap % 9) * channels : (tap % 9 + 1) * channels] = weight(tap)
 
     def lay_backward(target, weight):
-        group_size = max(1, LANES // n)
-        for a in range(3):
-            for j in range(0, 9, group_size):
-                taps = min(group_size, 9 - j)
-                piece_of = weight[pl.ds(9 * a + j, taps)].reshape(taps * n, channels)
-                target[a, :, j * n : (j + taps) * n] = piece_of.T
-
-    def convolve(weight, stack, emit, reverse=False):
+        for tap in range(27):
+            target[tap // 9, :, (tap % 9) * channels : (tap % 9 + 1) * channels] = weight(tap).T
+
+    def all_outputs(wall):
+        return lambda tap: jnp.concatenate([wall[q, tap * n : (tap + 1) * n, :] for q in range(nc)], axis=0)
+
+    def convolve(weight, height, stack, emit, reverse=False):
         def body(step, _):
             cols = pl.ds(pl.multiple_of(step * TILE, TILE), TILE)
             totals = [None] * planes
@@ -188,9 +186,8 @@
                     a = d + 2 - p if reverse else p - d
                     if 0 <= a < 3:
                         pairs.append((d, a))
-                left = jnp.concatenate([weight[a] for _, a in pairs], axis=0)
+                left = jnp.concatenate([weight(a) for _, a in pairs], axis=0)
                 term = jnp.dot(left, stack[p, :, cols], preferred_element_type=F32)
-                height = weight.shape[1]
                 for at, (d, _) in enumerate(pairs):
                     part = term[at * height : (at + 1) * height]
                     totals[d] = part if totals[d] is None else totals[d] + part
@@ -201,93 +198,18 @@
         lax.fori_loop(0, CELLS // TILE, body, 0)
 
     def filter_grad(total_ref, stack, padded):
-        count = stack.shape[1]
+        count = 9 * n
         for a in range(3):
             total = None
             for d in range(planes):
-                term = lax.dot_general(stack[d + 1], padded[d + a], (((1,), (1,)), ((), ())),
-                                       preferred_element_type=F32)
+                left = jnp.concatenate(
+                    [stack[d + 1, pl.ds(pl.multiple_of(j * channels + ci * n, n), n), :] for j in range(9)], axis=0)
+                term = lax.dot_general(left, padded[d + a], (((1,), (1,)), ((), ())), preferred_element_type=F32)
                 total = term if total is None else total + term
             total_ref[pl.ds(a * count, count), :] = total
         rest = ns * shard - 3 * count
         if rest:
             total_ref[pl.ds(3 * count, rest), :] = jnp.zeros((rest, channels), F32)
-
-    for d in range(planes):
-        xpad[1 + d, own, :] = to_blocks(x_ref[d])
-    for copy in gather_sends(xpad, sx, rx):
-        copy.start()
-    start_halo(xpad, own, sxh, rxh, 0)
-    for d in range(planes):
-        ctpad[1 + d] = to_blocks(ct_ref[d])
-    start_halo(ctpad, everything, sct, rct, 0)
-
-    lay_backward(bw2, w2_ref)
-    zero_edges(ctpad)
-    zero_edges(xpad)
-    for plane in range(1, planes + 1):
-        build(st_ct, ctpad, plane, -1)
-    wait_halo(ctpad, everything, sct, rct, 0)
-    build(st_ct, ctpad, 0, -1)
-    build(st_ct, ctpad, planes + 1, -1)
-
-    def reverse_parts(weight_t, stack, sums, outgoing, incoming, ssem, rsem):
-        def keep(d, cols, total):
-            sums[d, :, cols] = total
-
-        convolve(weight_t, stack, keep, reverse=True)
-        for k in range(1, nc):
-            target = lax.rem(ci + k, nc)
-            outgoing[k - 1] = sums[:, rows_of(target), :].astype(outgoing.dtype)
-            send(outgoing.at[k - 1], incoming.at[k - 1], ssem.at[k - 1], rsem.at[k - 1], "chan", target).start()
-
-    def part_copies(outgoing, incoming, ssem, rsem):
-        return [send(outgoing.at[k - 1], incoming.at[k - 1], ssem.at[k - 1], rsem.at[k - 1],
-                     "chan", lax.rem(ci + k, nc)) for k in range(1, nc)]
-
-    reverse_parts(bw2, st_ct, gh, part_out, part_in, sgh, rgh)
-
-    lay_forward(fw1, w1_ref)
-    gather_and_forward(xpad, sx, rx, sxh, rxh)
-    for plane in range(1, planes + 1):
-        build(wide, xpad, plane)
-    for k in range(nc):
-        wait_halo(xpad, rows_of(lax.rem(ci + nc - k, nc)), sxh, rxh, k)
-    build(wide, xpad, 0)
-    build(wide, xpad, planes + 1)
-
-    def hidden_out(d, cols, total):
-        pre[d, :, cols] = total
-        hpad[d + 1, own, cols] = (total * jax.nn.sigmoid(total)).astype(BF16)
-
-    convolve(fw1, wide, hidden_out)
-    for copy in gather_sends(hpad, sh, rh):
-        copy.start()
-    start_halo(hpad, own, shh, rhh, 0)
-    zero_edges(hpad)
-    lay_backward(bw1, w1_ref)
-    lay_forward(fw2, w2_ref)
-    zero_edges(gppad)
-
-    for copy in part_copies(part_out, part_in, sgh, rgh):
-        copy.wait_recv()
-
-    def slope(step, _):
-        d = step // (n // 16)
-        rows = pl.ds(pl.multiple_of((step % (n // 16)) * 16, 16), 16)
-        total = gh[d, pl.ds(pl.multiple_of(ci * n + (step % (n // 16)) * 16, 16), 16), :]
-        for k in range(nc - 1):
-            total = total + part_in[k, d, rows, :].astype(F32)
-        values = pre[d, rows, :]
-        sigma = jax.nn.sigmoid(values)
-        gppad[d + 1, rows, :] = (total * (sigma * (1.0 + values * (1.0 - sigma)))).astype(BF16)
-        return 0
-
-    lax.fori_loop(0, planes * (n // 16), slope, 0)
-    start_halo(gppad, everything, sgp, rgp, 0)
-    for plane in range(1, planes + 1):
-        build(st_gp, gppad, plane, -1)
-    filter_grad(g1, st_gp, xpad)
 
     nx = ns // 2
     core, xi = lax.rem(si, 2), si // 2
@@ -410,68 +332,179 @@
 
     first = Reduction(0, g1, sums1, q1_ref)
     second = Reduction(1, g2, sums2, q2_ref)
+
+    class Filter:
+        def __init__(self, which, wall, k):
+            self.wall, self.k = wall, k
+            self.owner = lax.rem(ci + nc - k, nc)
+            self.result = wall.at[self.owner]
+            self.base = (which * nc + k) * (3 + ns + nz)
+
+        def copy(self, rows, at, axis, index):
+            ref = self.result.at[rows]
+            return send(ref, ref, sw.at[self.base + at], rw.at[self.base + at], axis, index)
+
+        def from_chan(self):
+            rows = span(core, xi, zi)
+            ref = self.wall.at[ci, rows]
+            return send(ref, ref, sw.at[self.base], rw.at[self.base], "chan", lax.rem(ci + self.k, nc))
+
+        def samp_gather(self, arriving):
+            return [self.copy(span(core, xi, lax.rem(zi + nz - m, nz) if arriving else zi), 1 + m,
+                              "samp", lax.rem(zi + m, nz)) for m in range(1, nz)]
+
+        def x_gather(self, arriving):
+            return [self.copy(span(core, lax.rem(xi + nx - m, nx) if arriving else xi), 1 + nz + m,
+                              "slab", 2 * lax.rem(xi + m, nx) + core) for m in range(1, nx)]
+
+        def core_gather(self, arriving):
+            return [self.copy(span(1 - core if arriving else core), 1 + nz + nx, "slab", 2 * xi + 1 - core)]
+
+        def zero(self):
+            self.from_chan().start()
+
+        def one(self):
+            rows = span(core, xi, zi)
+            ref = self.wall.at[self.owner, rows]
+            send(ref, ref, sw.at[self.base], rw.at[self.base], "chan", lax.rem(ci + self.k, nc)).wait_recv()
+            for copy in self.samp_gather(False):
+                copy.start()
+
+        def two(self):
+            for copy in self.samp_gather(True):
+                copy.wait_recv()
+            for copy in self.x_gather(False):
+                copy.start()
+
+        def three(self):
+            for copy in self.x_gather(True):
+                copy.wait_recv()
+            for copy in self.core_gather(False):
+                copy.start()
+
+        def four(self):
+            for copy in self.core_gather(True):
+                copy.wait_recv()
+
+        def finish(self):
+            for copy in [self.from_chan()] + self.samp_gather(False) + self.x_gather(False) + self.core_gather(False):
+                copy.wait_send()
+
+    ones = [Filter(0, wall1, k) for k in range(1, nc)]
+    twos = [Filter(1, wall2, k) for k in range(1, nc)]
+
+    for wall, w_ref in ((wall1, w1_ref), (wall2, w2_ref)):
+        wall[ci, 0 : 27 * n, :] = w_ref[...].reshape(27 * n, channels)
+        if ns * shard > 27 * n:
+            wall[ci, 27 * n : ns * shard, :] = jnp.zeros((ns * shard - 27 * n, channels), BF16)
+    for item in ones + twos:
+        item.zero()
+    for d in range(planes):
+        xpad[1 + d, own, :] = to_blocks(x_ref[d])
+    for copy in gather_sends(xpad, sx, rx):
+        copy.start()
+    start_halo(xpad, own, sxh, rxh, 0)
+    for d in range(planes):
+        ctpad[1 + d, own, :] = to_blocks(ct_ref[d])
+    for copy in gather_sends(ctpad, sct, rct):
+        copy.start()
+    start_halo(ctpad, own, scth, rcth, 0)
+    zero_edges(xpad)
+    zero_edges(ctpad)
+    zero_edges(hpad)
+    zero_edges(gppad)
+    lay_forward(fw2, lambda tap: w2_ref[tap])
+    for item in ones + twos:
+        item.one()
+    for item in ones + twos:
+        item.two()
+    gather_and_forward(xpad, sx, rx, sxh, rxh)
+    for plane in range(1, planes + 1):
+        build(wide, xpad, plane)
+    for item in ones + twos:
+        item.three()
+    for k in range(nc):
+        wait_halo(xpad, rows_of(lax.rem(ci + nc - k, nc)), sxh, rxh, k)
+    build(wide, xpad, 0)
+    build(wide, xpad, planes + 1)
+    for item in ones:
+        item.four()
+    lay_forward(fw1, all_outputs(wall1))
+
+    def hidden_out(d, cols, total):
+        pre[d, :, cols] = total
+        hpad[d + 1, :, cols] = (total * jax.nn.sigmoid(total)).astype(BF16)
+
+    convolve(lambda a: fw1[a], channels, wide, hidden_out)
+    start_halo(hpad, everything, shh, rhh, 0)
+    gather_and_forward(ctpad, sct, rct, scth, rcth)
+    for plane in range(1, planes + 1):
+        build(st_ct, ctpad, plane, -1)
+    wait_halo(hpad, everything, shh, rhh, 0)
+    filter_grad(g2, st_ct, hpad)
+    second.one()
+    for item in twos:
+        item.four()
+    lay_backward(bw2, all_outputs(wall2))
+    for k in range(nc):
+        wait_halo(ctpad, rows_of(lax.rem(ci + nc - k, nc)), scth, rcth, k)
+    build(st_ct, ctpad, 0, -1)
+    build(st_ct, ctpad, planes + 1, -1)
+    second.two()
+
+    def slope(d, cols, total):
+        values = pre[d, :, cols]
+        sigma = jax.nn.sigmoid(values)
+        gppad[d + 1, :, cols] = (total * (sigma * (1.0 + values * (1.0 - sigma)))).astype(BF16)
+
+    convolve(lambda a: bw2[a], channels, st_ct, slope, reverse=True)
+    start_halo(gppad, everything, sgp, rgp, 0)
+    for plane in range(1, planes + 1):
+        build(st_gp, gppad, plane, -1)
+    second.three()
+    filter_grad(g1, st_gp, xpad)
     first.one()
-
+    lay_backward(bw1, all_outputs(wall1))
+    second.four()
+    first.two()
+    for plane in range(planes + 2):
+        build(wide, hpad, plane)
+    second.five()
+    first.three()
+
+    def block(d, cols, total):
+        result[d, :, cols] = (xpad[1 + d, own, cols].astype(F32) + total).astype(BF16)
+
+    convolve(lambda a: fw2[a], n, wide, block)
+    second.six()
+    first.four()
+    for d in range(planes):
+        out_ref[d] = from_blocks(result[d])
     wait_halo(gppad, everything, sgp, rgp, 0)
     build(st_gp, gppad, 0, -1)
     build(st_gp, gppad, planes + 1, -1)
-    reverse_parts(bw1, st_gp, back, back_out, back_in, sbk, rbk)
-
-    first.two()
-    gather_and_forward(hpad, sh, rh, shh, rhh)
-    for k in range(nc):
-        wait_halo(hpad, rows_of(lax.rem(ci + nc - k, nc)), shh, rhh, k)
-    filter_grad(g2, st_ct, hpad)
-    second.one()
-    first.three()
-    for plane in range(planes):
-        build(wide, hpad, plane)
-    second.two()
-    for plane in range(planes, planes + 2):
-        build(wide, hpad, plane)
-
-    def block(d, cols, total):
-        result[d, :, cols] = (xpad[1 + d, own, cols].astype(F32) + total).astype(BF16)
-
-    first.four()
-    convolve(fw2, wide, block)
-    second.three()
     first.five()
+
+    def volume_grad(d, cols, total):
+        result[d, :, cols] = (ctpad[1 + d, own, cols].astype(F32) + total).astype(BF16)
+
+    convolve(lambda a: bw1[a, own, :], n, st_gp, volume_grad, reverse=True)
+    first.six()
     for d in range(planes):
-        out_ref[d] = from_blocks(result[d])
-
-    for copy in part_copies(back_out, back_in, sbk, rbk):
-        copy.wait_recv()
-
-    def volume_grad(step, _):
-        d = step // (n // 16)
-        rows = pl.ds(pl.multiple_of((step % (n // 16)) * 16, 16), 16)
-        total = back[d, pl.ds(pl.multiple_of(ci * n + (step % (n // 16)) * 16, 16), 16), :]
-        for k in range(nc - 1):
-            total = total + back_in[k, d, rows, :].astype(F32)
-        gv_ref[d, rows, :] = from_blocks((ctpad[d + 1, rows, :].astype(F32) + total).astype(BF16))
-        return 0
-
-    lax.fori_loop(0, planes * (n // 16), volume_grad, 0)
-    second.four()
-    first.six()
-    second.five()
-    second.six()
+        gv_ref[d] = from_blocks(result[d])
+    second.seven()
     first.seven()
-    second.seven()
-
-    for copy in gather_sends(xpad, sx, rx) + gather_sends(hpad, sh, rh):
-        copy.wait_send()
-    for copy in part_copies(part_out, part_in, sgh, rgh) + part_copies(back_out, back_in, sbk, rbk):
+
+    for copy in gather_sends(xpad, sx, rx) + gather_sends(ctpad, sct, rct):
         copy.wait_send()
     for k in range(nc):
         rows = rows_of(lax.rem(ci + nc - k, nc))
         finish_halo(xpad, rows, sxh, rxh, k)
-        finish_halo(hpad, rows, shh, rhh, k)
-    finish_halo(ctpad, everything, sct, rct, 0)
+        finish_halo(ctpad, rows, scth, rcth, k)
+    finish_halo(hpad, everything, shh, rhh, 0)
     finish_halo(gppad, everything, sgp, rgp, 0)
-    first.finish()
-    second.finish()
+    for item in ones + twos + [first, second]:
+        item.finish()
 
 
 def per_device(volume, cotangent, filter_one, filter_two):
@@ -500,27 +533,26 @@
             pltpu.VMEM((nx - 1, shard, channels), two)] * 2 + [
             pltpu.VMEM((nz - 1, piece, channels), three)] * 2
 
-    scratch = [pltpu.VMEM((3, n, 9 * channels), BF16)] * 2 + [pltpu.VMEM((3, channels, 9 * n), BF16)] * 2 + [
+    stack = pltpu.VMEM((padded, 9 * channels, cells), BF16)
+    plane_buffer = pltpu.VMEM((padded, channels, cells), BF16)
+    scratch = [
+        pltpu.VMEM((3, channels, 9 * channels), BF16),
+        pltpu.VMEM((3, n, 9 * channels), BF16),
+        pltpu.VMEM((3, channels, 9 * channels), BF16),
+        pltpu.VMEM((3, channels, 9 * channels), BF16),
+        pltpu.VMEM((nc, rows, channels), BF16),
+        pltpu.VMEM((nc, rows, channels), BF16),
         pltpu.VMEM((planes, n, cells), BF16),
-        pltpu.VMEM((padded, channels, cells), BF16),
-        pltpu.VMEM((padded, channels, cells), BF16),
-        pltpu.VMEM((padded, n, cells), BF16),
-        pltpu.VMEM((padded, n, cells), BF16),
-        pltpu.VMEM((padded, 9 * channels, cells), BF16),
-        pltpu.VMEM((padded, 9 * n, cells), BF16),
-        pltpu.VMEM((padded, 9 * n, cells), BF16),
-        pltpu.VMEM((planes, n, cells), F32),
+        plane_buffer, plane_buffer, plane_buffer, plane_buffer, stack, stack, stack,
         pltpu.VMEM((planes, channels, cells), F32),
-        pltpu.VMEM((planes, channels, cells), F32),
-    ] + [pltpu.VMEM((nc - 1, planes, n, cells), BF16)] * 4 + [
         pltpu.VMEM((rows, channels), F32),
         pltpu.VMEM((rows, channels), F32),
         reduction_buffers(SUM_TYPES[0]),
         reduction_buffers(SUM_TYPES[1]),
         dma((planes * nc,)), dma((planes * nc,)), dma((2 * nc,)), dma((2 * nc,)),
-        dma((2,)), dma((2,)), dma((nc,)), dma((nc,)),
         dma((planes * nc,)), dma((planes * nc,)), dma((2 * nc,)), dma((2 * nc,)),
-        dma((2,)), dma((2,)), dma((nc,)), dma((nc,)),
+        dma((2,)), dma((2,)), dma((2,)), dma((2,)),
+        dma((2 * nc * (3 + ns + nz),)), dma((2 * nc * (3 + ns + nz),)),
         dma((4 * (1 + ns + nz),)), dma((4 * (1 + ns + nz),)),
     ]
     sizes = (nz, ns, nc, n, planes, shard, piece, norm_scale)

time: 68.2 us -> 70.5 us (1.034)
  Pallas kernels: 60.3 us -> 62.5 us
    pallas_call x1, Pallas kernels: 60.3 us -> 62.5 us  [per_device(): pl.pallas_call(functools.partial(kernel, sizes), out_shape=(jax.ShapeDtyp...]
where the time goes in v4:
time: 70.5 us; the launch traced here: 70.2 us
  Pallas kernels  62.5 us (89%)
  local copies, waits for them, and re-layouts  5.02 us (7%)
  other arithmetic  2.02 us (3%)
    pallas_call x1, Pallas kernels, per_device(): pl.pallas_call(functools.partial(kernel, sizes), out_shape=(jax.ShapeDtyp...  62.5 us
    unnamed x8, local copies, waits for them, and re-layouts  3.02 us
    convert_element_type x2, other arithmetic, filter_out(): jnp.transpose(values, (2, 0, 1, 3)).reshape(n, 27, channels).astype(F32)  2.02 us
    transpose x1, local copies, waits for them, and re-layouts, per_device(): ct = jnp.transpose(cotangent[0], (1, 0, 2))  1.94 us

profile of v4, /device:TPU:0, one launch (start us, length us, event | category | flops | bytes accessed | tf_op | source)
XLA Modules:
  0.0 70.2 jit_solution(5845399654303884287)
XLA Ops:
  0.6 1.9 %copy_bitcast_fusion = (bf16[2,64,1024]{2,1,0:T(8,128)(2,1)}, bf16[2,64,1024]{2,1,0:T(8,128)(2,1)}) fusion(bf16[1,64,2,1024]{3,2,1,0:T(2,128)(2,1)} %param.5, bf16[1,64,2,1024]{3,2,1,0:T(2,128)(2,1)} %param.4), kind=kLoop, calls=%fused_computation | loop fusion | bytes 1048576 | tf_op jit(solution)/shard_map/transpose | solution.py:523
  2.6 62.5 %residual_pair.1 = (bf16[2,64,1024]{2,1,0:T(8,128)(2,1)}, bf16[2,64,1024]{2,1,0:T(8,128)(2,1)}, bf16[1792,128]{1,0:T(8,128)(2,1)}, bf16[1792,128]{1,0:T(8,128)(2,1)}) custom-call(bf16[2,64,1024]{2,1,0:T(8,128)(2,1)} %get-tuple-element.17.x_ref, bf16[2,64,1024]{2,1,0:T(8,128)(2,1)} %get-tuple-element.16.ct_ref, bf16[27,64,128]{2,1,0:T(8,128)(2,1)} %bitcast.32, ...), custom_call_target="tpu_custom_call" | custom-call | flops 5435817984 | bytes 8388608 | tf_op jit(solution)/shard_map/residual_pair/pallas_call | solution.py:559
  65.1 0.0 copy-start.2
  65.1 0.0 copy-start.1
  65.1 2.0 %copy.10 = bf16[1,64,2,1024]{3,2,1,0:T(2,128)(2,1)} copy(bf16[1,64,2,1024]{3,1,2,0:T(8,128)(2,1)} %bitcast.31) | data formatting | bytes 524288
  67.1 0.0 copy-done.2
  67.1 1.0 %copy.11 = bf16[1,64,2,1024]{3,2,1,0:T(2,128)(2,1)} copy(bf16[1,64,2,1024]{3,1,2,0:T(8,128)(2,1)S(1)} %bitcast.30) | data formatting | bytes 524288
  68.1 0.0 copy-done.1
  68.1 0.0 copy-start
  68.1 1.0 %convert.6 = f32[3,9,64,128]{3,2,1,0:T(8,128)} convert(bf16[3,9,64,128]{3,2,1,0:T(8,128)(2,1)S(1)} %bitcast.26) | non-fusion elementwise | flops 221184 | bytes 1327104 | tf_op jit(solution)/shard_map/convert_element_type | solution.py:579
  69.1 0.0 copy-done
  69.2 1.0 %convert.7 = f32[3,9,64,128]{3,2,1,0:T(8,128)} convert(bf16[3,9,64,128]{3,2,1,0:T(8,128)(2,1)S(1)} %bitcast.27) | non-fusion elementwise | flops 221184 | bytes 1327104 | tf_op jit(solution)/shard_map/convert_element_type | solution.py:579
  (2 shorter events, 0.1 us)
Async XLA Ops:
  65.1 2.0 %copy-start.2 = (bf16[2,64,1024]{2,1,0:T(8,128)(2,1)S(1)}, bf16[2,64,1024]{2,1,0:T(8,128)(2,1)}, u32[]{:S(2)}) copy-start(bf16[2,64,1024]{2,1,0:T(8,128)(2,1)} %get-tuple-element.9) | copy-start | bytes 786436
  65.1 3.0 %copy-start.1 = (bf16[1792,128]{1,0:T(8,128)(2,1)S(1)}, bf16[1792,128]{1,0:T(8,128)(2,1)}, u32[]{:S(2)}) copy-start(bf16[1792,128]{1,0:T(8,128)(2,1)} %get-tuple-element.10) | copy-start | bytes 1376260
  68.1 1.1 %copy-start = (bf16[1792,128]{1,0:T(8,128)(2,1)S(1)}, bf16[1792,128]{1,0:T(8,128)(2,1)}, u32[]{:S(2)}) copy-start(bf16[1792,128]{1,0:T(8,128)(2,1)} %get-tuple-element.11) | copy-start | bytes 1376260
